TPU v7x, 512 devices: a whole 4x8x8 slice. The times are simulated.
512 devices in a mesh: member: 32 (over x, z), patch: 16 (over y, core).
Axes of the slice: x: 4, y: 8, z: 8, core: 2. Of those that a mesh axis runs over, the one named last changes fastest.
Arguments:
- background_fields: bfloat16 [512, 960, 384], P('patch', 'member')
- measured_location: int32 [512, 640], P('patch'), may hold values from 0 to 767
- measured_datum: float32 [512, 640], P('patch'), may hold values from -6 to 6
- measured_error_spread: float32 [512, 640], P('patch'), may hold values from 0.3 to 3
- measured_distance_band: int32 [512, 640], P('patch'), may hold values from 0 to 15
- measured_tally: int32 [512], P('patch'), may hold values from 160 to 640, as said below
- taper_weights: int32 [16], replicated, may hold values from 8 to 64
Outputs:
- analysis: bfloat16 [512, 960, 384], P('patch', 'member')
Inputs may be any that keep to these rules, and one draw needn't show every extreme that they name: `measured_tally`: the live observations of a patch fill its first slots; at least one patch fills all 640.
All inputs are finite; a program needn't handle non-finite values.
Results may differ from a plain program's by a relative error of at most 0.006.
Values may be sent and summed in bfloat16 or wider, within the bound.
No kernel may reach another device: no remote copies, remote signals or barrier semaphores. Data moves between devices by JAX's collectives and lax.ppermute only.
A program may use at most 64 MiB of HBM per device.

v0:
```python
import jax
import jax.numpy as jnp
import numpy as np
from jax import lax
from jax.experimental import pallas as pl
from jax.experimental.pallas import tpu as pltpu
from jax.sharding import PartitionSpec as P

STRATUM_PAIRS = 24
PIECE_WIDTH = 16
FRINGE_REACH = 8
NCLASS = 16
CORE = STRATUM_PAIRS * PIECE_WIDTH
RIM = STRATUM_PAIRS * FRINGE_REACH
SPAN = CORE + 2 * RIM
OBS = 640
GROUP = 32
HELD = 30
PADDED = 32
ROWS = GROUP * PADDED
MEMBERS = GROUP * HELD
HALF = 16
TILE = 256

F32 = jnp.float32
BF16 = jnp.bfloat16
I32 = jnp.int32

CYCLES = (
    (0, 8, 9, 17, 16, 23, 22, 14, 15, 7, 6, 5, 13, 21, 20, 12,
     4, 3, 2, 1, 25, 26, 18, 10, 11, 19, 27, 28, 29, 30, 31, 24),
    (0, 1, 9, 10, 2, 26, 27, 3, 11, 12, 13, 14, 6, 30, 22, 21,
     29, 5, 4, 28, 20, 19, 18, 17, 25, 24, 16, 8, 15, 23, 31, 7),
)
HOMES = np.array(CYCLES, np.int32).reshape(-1)
HOSTED = np.argsort(np.array(CYCLES, np.int32), axis=1).astype(np.int32).reshape(-1)


def vmem():
    return pl.BlockSpec(memory_space=pltpu.VMEM)


def smem():
    return pl.BlockSpec(memory_space=pltpu.SMEM)


def params():
    return pltpu.CompilerParams(vmem_limit_bytes=40 * 1024 * 1024)


def shape(*dims, dtype=BF16):
    return jax.ShapeDtypeStruct(dims, dtype)


def mm(a, b):
    return jnp.dot(a, b, preferred_element_type=F32)


def mm_nt(a, b):
    return lax.dot_general(a, b, (((1,), (1,)), ((), ())), preferred_element_type=F32)


def swap_matrix(rows, columns, inner):
    row = lax.broadcasted_iota(I32, (rows, columns), 0)
    column = lax.broadcasted_iota(I32, (rows, columns), 1)
    outer = rows // inner
    wanted = (row & (inner - 1)) * outer + row // inner
    return jnp.where(column == wanted, 1.0, 0.0).astype(BF16)


def entry_kernel(place, homes, states, out):
    first = place[0] * GROUP
    swap = swap_matrix(GROUP * HALF, GROUP * HALF, HALF)
    for start in (0, HALF):
        count = min(HALF, HELD - start)
        block = states[start : start + count].reshape(count * GROUP, CORE)
        moved = mm(swap[:, : count * GROUP], block).astype(BF16)
        for p in range(GROUP):
            out[homes[first + p], start : start + HALF, :] = moved[p * HALF : (p + 1) * HALF, :]


def exit_kernel(place, homes, analysed, out, ordered):
    first = place[0] * GROUP
    swap = swap_matrix(GROUP * HALF, GROUP * HALF, GROUP)
    for start in (0, HALF):
        count = min(HALF, HELD - start)
        for p in range(GROUP):
            ordered[p * HALF : (p + 1) * HALF, :] = analysed[homes[first + p], start : start + HALF, :]
        moved = mm(swap[: count * GROUP, :], ordered[...]).astype(BF16)
        out[start : start + count] = moved.reshape(count, GROUP, CORE)


def prepare_kernel(
    place, hosted, tally, taper, location, datum, error_spread, band,
    root_column, ratio_column, root_row, pick,
):
    me = hosted[place[0] * GROUP + place[1]]
    mine = pl.ds(me, 1)
    flat = location[mine, :]
    level = flat >> 5
    column = flat & 31
    spot = level * PIECE_WIDTH + column - FRINGE_REACH
    rim = level * FRINGE_REACH + (column & (FRINGE_REACH - 1))
    spot = jnp.where(column < FRINGE_REACH, CORE + rim, spot)
    spot = jnp.where(column >= FRINGE_REACH + PIECE_WIDTH, CORE + RIM + rim, spot)

    classes = band[mine, :]
    weight = jnp.zeros(classes.shape, I32)
    for k in range(NCLASS):
        weight = jnp.where(classes == k, taper[k], weight)
    slot = lax.broadcasted_iota(I32, classes.shape, 1)
    live = jnp.where(slot < tally[me], 1.0, 0.0)
    precision = live * (weight.astype(F32) / 64.0) / error_spread[mine, :]
    pulled = precision * datum[mine, :]
    for t in range(0, SPAN, 128):
        hit = lax.broadcasted_iota(I32, (128, OBS), 0) + t == spot
        total = jnp.sum(jnp.where(hit, precision, 0.0), axis=1, keepdims=True)
        pull = jnp.sum(jnp.where(hit, pulled, 0.0), axis=1, keepdims=True)
        total = jnp.broadcast_to(total, (128, 128))
        pull = jnp.broadcast_to(pull, (128, 128))
        root = jnp.sqrt(total)
        root_column[t : t + 128, :] = root
        ratio_column[t : t + 128, :] = jnp.where(
            total > 0.0, pull / jnp.where(total > 0.0, root, 1.0), 0.0
        )
        root_row[:, t : t + 128] = root.T[0:8, :]

    row = lax.broadcasted_iota(I32, (2 * RIM, CORE), 0)
    lane = lax.broadcasted_iota(I32, (2 * RIM, CORE), 1)
    rim = jnp.where(row < RIM, row, row - RIM)
    source = (rim >> 3) * PIECE_WIDTH + (rim & (FRINGE_REACH - 1))
    source = jnp.where(row < RIM, source + PIECE_WIDTH - FRINGE_REACH, source)
    pick[...] = jnp.where(lane == source, 1.0, 0.0).astype(BF16)


def extract_kernel(states, pick, rightward, leftward):
    for t in range(0, ROWS, TILE):
        rims = mm_nt(pick[...], states[t : t + TILE, :]).astype(BF16)
        rightward[:, t : t + TILE] = rims[:RIM, :]
        leftward[:, t : t + TILE] = rims[RIM:, :]


def own_kernel(
    states, root_column, ratio_column, root_row,
    spread, state_mean, gram, basis, pulls, sums,
):
    total = jnp.zeros((1, CORE), F32)
    for t in range(0, ROWS, TILE):
        total += jnp.sum(states[t : t + TILE, :].astype(F32), axis=0, keepdims=True)
    mean = total / MEMBERS
    state_mean[...] = jnp.broadcast_to(mean, (8, CORE))
    live = (lax.broadcasted_iota(I32, (TILE, CORE), 0) & (PADDED - 1)) < HELD
    covariance = jnp.zeros((CORE, CORE), F32)
    for t in range(0, ROWS, TILE):
        tile = jnp.where(live, states[t : t + TILE, :].astype(F32) - mean, 0.0)
        spread[t : t + TILE, :] = tile.astype(BF16)
        covariance += mm(tile.T.astype(BF16), tile.astype(BF16))
    squares = jnp.zeros((1, 1), F32)
    trace = jnp.zeros((1, 1), F32)
    corner = lax.broadcasted_iota(I32, (128, 128), 0) == lax.broadcasted_iota(I32, (128, 128), 1)
    column_mean = jnp.broadcast_to(mean, (128, CORE)).T
    for t in range(0, CORE, 128):
        root = root_column[t : t + 128, :]
        lifted = jnp.tile(root, (1, CORE // 128)) * covariance[t : t + 128, :]
        basis[t : t + 128, :] = lifted
        block = lifted * root_row[0:1, :CORE]
        gram[t : t + 128, :] = block.astype(BF16)
        squares += jnp.sum(block * block, keepdims=True)
        trace += jnp.sum(jnp.where(corner, block[:, t : t + 128], 0.0), keepdims=True)
        pulls[t : t + 128, :] = ratio_column[t : t + 128, :] - root * column_mean[t : t + 128, :]
    sums[0:8, :] = jnp.broadcast_to(squares, (8, 128))
    sums[8:16, :] = jnp.broadcast_to(trace, (8, 128))


def analyse_kernel(
    before, after, spread, state_mean, own_gram, own_basis, own_pulls, sums,
    root_column, ratio_column, root_row,
    out, fringe_t, fringe, gram, basis, pulls,
):
    live = (lax.broadcasted_iota(I32, (RIM, ROWS), 1) & (PADDED - 1)) < HELD
    for rims, top in ((before, 0), (after, RIM)):
        rows = slice(top, top + RIM)
        tile = rims[...].astype(F32)
        mean = jnp.sum(tile, axis=1, keepdims=True) / MEMBERS
        tile = jnp.where(live, tile - mean, 0.0)
        fringe_t[rows, :] = tile.astype(BF16)
        fringe[:, rows] = tile.T.astype(BF16)
        span = slice(CORE + top, CORE + top + RIM)
        pulls[span, :] = ratio_column[span, :] - root_column[span, :] * mean
    pulls[:CORE, :] = own_pulls[...]
    gram[:CORE, :CORE] = own_gram[...]
    basis[:CORE, :] = own_basis[...]

    squares = sums[0:1, 0:1]
    trace = sums[8:9, 0:1]
    corner = lax.broadcasted_iota(I32, (128, 128), 0) == lax.broadcasted_iota(I32, (128, 128), 1)
    for t in range(0, CORE, 128):
        root = root_column[CORE + t : CORE + t + 128, :]
        root = jnp.tile(root, (1, CORE // 128))
        lifted = root * mm(fringe_t[t : t + 128, :], spread[...])
        basis[CORE + t : CORE + t + 128, :] = lifted
        block = lifted * root_row[0:1, :CORE]
        gram[CORE + t : CORE + t + 128, :CORE] = block.astype(BF16)
        gram[:CORE, CORE + t : CORE + t + 128] = block.T.astype(BF16)
        squares += 2.0 * jnp.sum(block * block, keepdims=True)
        block = root * mm(fringe_t[t : t + 128, :], fringe[...]) * root_row[0:1, CORE:]
        gram[CORE + t : CORE + t + 128, CORE:] = block.astype(BF16)
        squares += jnp.sum(block * block, keepdims=True)
        trace += jnp.sum(jnp.where(corner, block[:, t : t + 128], 0.0), keepdims=True)
    draw = F32(MEMBERS - 1)
    inverse = 1.0 / (draw + 2.0 * squares / (draw + trace))

    a = draw * inverse
    r = 1.5 - 0.5 * a
    s = 1.5 - 0.5 * a * r * r
    z = basis[...] * inverse
    d = pulls[...]

    def step(*parts):
        both = jnp.concatenate(parts, axis=1).astype(BF16)
        product = mm(gram[...], both) * inverse
        return product[:, :CORE], product[:, CORE:]

    v = -0.5 * z
    pv, px = step(v, d)
    v = 2.0 * r * v - 0.5 * pv
    x = r * d - 0.5 * px
    pv, px = step(v, x)
    v = -0.5 * (r * r * z + a * v + pv)
    x = r * x - 0.5 * px
    pv, px = step(v, x)
    v = r * v - 0.5 * s * z - 0.5 * pv
    x = 1.5 * d - 0.5 * (a * x + px)
    x = r * x - 0.5 * inverse * mm(gram[...], x.astype(BF16))
    y = inverse * mm(gram[...], x.astype(BF16))
    shift = []
    for t in range(0, CORE, 128):
        both = r * s * x * z[:, t : t + 128] + y * v[:, t : t + 128]
        shift.append(jnp.sum(both, axis=0, keepdims=True))
    base = state_mean[0:1, :] + jnp.concatenate(shift, axis=1)
    lift = (jnp.tile(root_column[...], (1, CORE // 128)) * v).astype(BF16)
    gain = jnp.sqrt(a)
    for t in range(0, ROWS, TILE):
        own = spread[t : t + TILE, :]
        moved = mm(own, lift[:CORE, :]) + mm(fringe[t : t + TILE, :], lift[CORE:, :])
        moved += r * s * own.astype(F32)
        out[t : t + TILE, :] = (base + gain * moved).astype(BF16)


def call(kernel, name, smems, vmems, out_shape, scratch_shapes=(), flops=0):
    return pl.pallas_call(
        kernel,
        in_specs=[smem()] * smems + [vmem()] * vmems,
        out_specs=jax.tree.map(lambda _: vmem(), out_shape),
        out_shape=out_shape,
        scratch_shapes=list(scratch_shapes),
        compiler_params=params(),
        cost_estimate=pl.CostEstimate(flops=flops, bytes_accessed=1 << 20, transcendentals=0),
        name=name,
    )


def enter(place, homes, states):
    return call(
        entry_kernel, "entry", 2, 1, shape(GROUP, PADDED, CORE), flops=4 * 512 * 512 * CORE
    )(place, homes, states)


def leave(place, homes, analysed):
    return call(
        exit_kernel, "exit", 2, 1, shape(HELD, GROUP, CORE),
        [pltpu.VMEM((GROUP * HALF, CORE), BF16)], 4 * 512 * 512 * CORE,
    )(place, homes, analysed)


def prepare(place, hosted, tally, taper, location, datum, error_spread, band):
    return call(
        prepare_kernel, "prepare", 4, 4,
        [shape(SPAN, 128, dtype=F32), shape(SPAN, 128, dtype=F32), shape(8, SPAN, dtype=F32),
         shape(2 * RIM, CORE)],
        flops=4 * SPAN * OBS,
    )(place, hosted, tally, taper, location, datum, error_spread, band)


def extract(states, pick):
    return call(
        extract_kernel, "extract", 0, 2, [shape(RIM, ROWS), shape(RIM, ROWS)],
        flops=4 * RIM * CORE * ROWS,
    )(states, pick)


def own_part(states, root_column, ratio_column, root_row):
    return call(
        own_kernel, "own_part", 0, 4,
        [shape(ROWS, CORE), shape(8, CORE, dtype=F32), shape(CORE, CORE),
         shape(CORE, CORE, dtype=F32), shape(CORE, 128, dtype=F32), shape(16, 128, dtype=F32)],
        flops=2 * ROWS * CORE * CORE,
    )(states, root_column, ratio_column, root_row)


def analyse(before, after, own, prepared):
    return call(
        analyse_kernel, "analyse", 0, 11, shape(ROWS, CORE),
        [
            pltpu.VMEM((CORE, ROWS), BF16),
            pltpu.VMEM((ROWS, CORE), BF16),
            pltpu.VMEM((SPAN, SPAN), BF16),
            pltpu.VMEM((SPAN, CORE), F32),
            pltpu.VMEM((SPAN, 128), F32),
        ],
        8 * SPAN * SPAN * CORE,
    )(before, after, *own, *prepared)


def local(
    background_fields,
    measured_location,
    measured_datum,
    measured_error_spread,
    measured_distance_band,
    measured_tally,
    taper_weights,
):
    axes = ("member", "patch")
    groups = lax.axis_size("patch")
    place = jnp.stack([lax.axis_index("patch") % 2, lax.axis_index("member")]).astype(I32)
    homes = jnp.asarray(HOMES)
    sent = enter(place, homes, jnp.transpose(background_fields, (1, 0, 2)))
    received = lax.all_to_all(sent, "member", split_axis=0, concat_axis=0, tiled=True)
    *prepared, pick = prepare(
        place, jnp.asarray(HOSTED), measured_tally, taper_weights, measured_location,
        measured_datum, measured_error_spread, measured_distance_band,
    )
    states = received.reshape(ROWS, CORE)
    rightward, leftward = extract(states, pick)
    owners = [CYCLES[g % 2][p] * groups + g for g in range(groups) for p in range(GROUP)]
    up = list(zip(owners, owners[1:] + owners[:1]))
    down = [(j, i) for i, j in up]
    before = lax.ppermute(rightward, axes, up)
    after = lax.ppermute(leftward, axes, down)
    own = own_part(states, *prepared)
    analysed = analyse(before, after, own, prepared).reshape(GROUP, PADDED, CORE)
    returned = lax.all_to_all(analysed, "member", split_axis=0, concat_axis=0, tiled=True)
    return jnp.transpose(leave(place, homes, returned), (1, 0, 2))


def solution(mesh):
    placed = (
        P("patch", "member", None),
        P("patch", None),
        P("patch", None),
        P("patch", None),
        P("patch", None),
        P("patch"),
        P(),
    )
    return jax.shard_map(
        local, mesh=mesh, in_specs=placed, out_specs=P("patch", "member", None), check_vma=False
    )
```

profile of v0, /device:TPU:25, one launch (start us, length us, event | category | flops | bytes accessed | tf_op | source)
XLA Modules:
  0.0 92.9 jit_solution(1318144304168204046)
XLA Ops:
  0.0 0.1 pad_add_fusion.place
  0.1 0.0 copy-start.5
  0.1 0.7 copy-done.5
  0.7 0.0 copy-start
  0.7 1.1 %copy-done = bf16[32,30,384]{2,0,1:T(8,128)(2,1)S(1)} copy-done((bf16[32,30,384]{2,0,1:T(8,128)(2,1)S(1)}, bf16[32,30,384]{2,0,1:T(8,128)(2,1)}, u32[]{:S(2)}) %copy-start) | copy-done | bytes 737304
  1.8 2.2 %entry.1 = bf16[32,32,384]{2,1,0:T(8,128)(2,1)} custom-call(s32[2]{0:T(128)S(1)} %pad_add_fusion.place, s32[64]{0:T(128)S(1)} %copy-done.5, bf16[30,32,384]{2,1,0:T(8,128)(2,1)S(1)} %bitcast.9), custom_call_target="tpu_custom_call" | custom-call | flops 402653184 | bytes 1048576 | tf_op jit(solution)/shard_map/entry/pallas_call | solution.py:264
  4.0 0.0 copy-start.1
  4.0 0.0 copy-start.2
  4.0 0.0 copy-start.3
  4.0 0.0 copy-start.4
  4.0 0.0 copy-start.6
  4.0 0.0 copy-start.7
  4.0 0.0 copy-start.8
  4.1 13.0 %all-to-all-start = ((bf16[32,32,384]{2,1,0:T(8,128)(2,1)}), bf16[32,32,384]{2,1,0:T(8,128)(2,1)S(1)}, u32[]{:S(2)}, u32[]{:S(2)}) async-start(bf16[32,32,384]{2,1,0:T(8,128)(2,1)} %entry.1), calls=%async_computation | async-start | bytes 1572864 | tf_op jit(solution)/shard_map/all_to_all | solution.py:329
  17.1 0.0 copy-done.1
  17.1 0.0 copy-done.2
  17.1 0.0 copy-done.3
  17.1 0.0 copy-done.4
  17.1 0.0 copy-done.6
  17.1 0.0 copy-done.7
  17.2 0.0 copy-done.8
  17.2 1.3 %prepare.1 = (f32[768,128]{1,0:T(8,128)S(1)}, f32[768,128]{1,0:T(8,128)S(1)}, f32[8,768]{1,0:T(8,128)S(1)}, bf16[384,384]{1,0:T(8,128)(2,1)S(1)}) custom-call(s32[2]{0:T(128)S(1)} %pad_add_fusion.place, s32[64]{0:T(128)S(1)} %copy-done.8, s32[32]{0:T(128)S(1)} %copy-done.6, s32[16]{0:T(128)S(1)} %copy-done.7, s32[32,640]{1,0:T(8,128)S(1)} %copy-done.1, ...), custom_call_target="tpu_custom_call" | custom-call | flops 1966080 | bytes 1048576 | tf_op jit(solution)/shard_map/prepare/pallas_call | solution.py:277
  18.5 17.9 %all-to-all-done = bf16[32,32,384]{2,1,0:T(8,128)(2,1)S(1)} async-done(((bf16[32,32,384]{2,1,0:T(8,128)(2,1)}), bf16[32,32,384]{2,1,0:T(8,128)(2,1)S(1)}, u32[]{:S(2)}, u32[]{:S(2)}) %all-to-all-start) | async-done | bytes 786464 | tf_op jit(solution)/shard_map/all_to_all | solution.py:329
  36.4 0.6 extract.1
  37.0 5.4 %collective-permute-start = (bf16[192,1024]{1,0:T(8,128)(2,1)S(1)}, bf16[192,1024]{1,0:T(8,128)(2,1)S(1)}, u32[]{:S(2)}, u32[]{:S(2)}) collective-permute-start(bf16[192,1024]{1,0:T(8,128)(2,1)S(1)} %get-tuple-element.18), channel_id=1, source_target_pairs={{0,128},{128,144},{144,272},{272,256},{256,368},{368,352},{352,224... | collective-permute-start | bytes 1179656 | tf_op jit(solution)/shard_map/ppermute | solution.py:339
  42.3 3.9 %collective-permute-start.1 = (bf16[192,1024]{1,0:T(8,128)(2,1)S(1)}, bf16[192,1024]{1,0:T(8,128)(2,1)S(1)}, u32[]{:S(2)}, u32[]{:S(2)}) collective-permute-start(bf16[192,1024]{1,0:T(8,128)(2,1)S(1)} %get-tuple-element.19), channel_id=1, source_target_pairs={{128,0},{144,128},{272,144},{256,272},{368,256},{352,368},{224,352... | collective-permute-start | bytes 1179656 | tf_op jit(solution)/shard_map/ppermute | solution.py:340
  46.3 0.9 %own_part.1 = (bf16[1024,384]{1,0:T(8,128)(2,1)S(1)}, f32[8,384]{1,0:T(8,128)S(1)}, bf16[384,384]{1,0:T(8,128)(2,1)S(1)}, f32[384,384]{1,0:T(8,128)S(1)}, f32[384,128]{1,0:T(8,128)S(1)}, /*index=5*/f32[16,128]{1,0:T(8,128)S(1)}) custom-call(bf16[1024,384]{1,0:T(8,128)(2,1)S(1)} %bitcast.7, f32[768,128]{1,0:T(8,128)S(1)} %get-tuple-element.20.root_column, ...), custom_call_target="tpu_custom_call" | custom-call | flops 301989888 | bytes 1048576 | tf_op jit(solution)/shard_map/own_part/pallas_call | solution.py:293
  47.2 2.9 %collective-permute-done.before = bf16[192,1024]{1,0:T(8,128)(2,1)S(1)} collective-permute-done((bf16[192,1024]{1,0:T(8,128)(2,1)S(1)}, bf16[192,1024]{1,0:T(8,128)(2,1)S(1)}, u32[]{:S(2)}, u32[]{:S(2)}) %collective-permute-start) | collective-permute-done | bytes 393248 | tf_op jit(solution)/shard_map/ppermute | solution.py:339
  50.1 1.0 %collective-permute-done.1.after = bf16[192,1024]{1,0:T(8,128)(2,1)S(1)} collective-permute-done((bf16[192,1024]{1,0:T(8,128)(2,1)S(1)}, bf16[192,1024]{1,0:T(8,128)(2,1)S(1)}, u32[]{:S(2)}, u32[]{:S(2)}) %collective-permute-start.1) | collective-permute-done | bytes 393248 | tf_op jit(solution)/shard_map/ppermute | solution.py:340
  51.1 6.3 %analyse.1 = bf16[1024,384]{1,0:T(8,128)(2,1)S(1)} custom-call(bf16[192,1024]{1,0:T(8,128)(2,1)S(1)} %collective-permute-done.before, bf16[192,1024]{1,0:T(8,128)(2,1)S(1)} %collective-permute-done.1.after, bf16[1024,384]{1,0:T(8,128)(2,1)S(1)} %get-tuple-element.23.spread, f32[8,384]{1,0:T(8,128)S(1)} %get-tuple-element.24.state_mean, ...), custom_call_target="tpu_custom_call" | custom-call | flops 1811939328 | bytes 1048576 | tf_op jit(solution)/shard_map/analyse/pallas_call | solution.py:302
  57.5 33.3 %all_to_all.10.analysed = bf16[32,32,384]{2,1,0:T(8,128)(2,1)S(1)} all-to-all(bf16[32,32,384]{2,1,0:T(8,128)(2,1)S(1)} %bitcast.8), channel_id=1, replica_groups=mesh['member'=32,'patch'=16] {'member'}, dimensions={0} | all-to-all | bytes 1572864 | tf_op jit(solution)/shard_map/all_to_all | solution.py:343
  90.7 2.1 %exit.1 = bf16[30,32,384]{2,1,0:T(8,128)(2,1)} custom-call(s32[2]{0:T(128)S(1)} %pad_add_fusion.place, s32[64]{0:T(128)S(1)} %copy-done.5, bf16[32,32,384]{2,1,0:T(8,128)(2,1)S(1)} %all_to_all.10.analysed), custom_call_target="tpu_custom_call" | custom-call | flops 402653184 | bytes 1048576 | tf_op jit(solution)/shard_map/exit/pallas_call | solution.py:270
Async XLA Ops:
  0.1 0.7 copy-start.5
  0.7 1.1 %copy-start = (bf16[32,30,384]{2,0,1:T(8,128)(2,1)S(1)}, bf16[32,30,384]{2,0,1:T(8,128)(2,1)}, u32[]{:S(2)}) copy-start(bf16[32,30,384]{2,0,1:T(8,128)(2,1)} %param.9) | copy-start | bytes 2211844
  4.0 13.1 %copy-start.1 = (s32[32,640]{1,0:T(8,128)S(1)}, s32[32,640]{1,0:T(8,128)}, u32[]{:S(2)}) copy-start(s32[32,640]{1,0:T(8,128)} %location.1) | copy-start | bytes 245764
  4.0 13.1 %copy-start.2 = (f32[32,640]{1,0:T(8,128)S(1)}, f32[32,640]{1,0:T(8,128)}, u32[]{:S(2)}) copy-start(f32[32,640]{1,0:T(8,128)} %datum.1) | copy-start | bytes 245764
  4.0 13.1 %copy-start.3 = (f32[32,640]{1,0:T(8,128)S(1)}, f32[32,640]{1,0:T(8,128)}, u32[]{:S(2)}) copy-start(f32[32,640]{1,0:T(8,128)} %error_spread.1) | copy-start | bytes 245764
  4.0 13.1 %copy-start.4 = (s32[32,640]{1,0:T(8,128)S(1)}, s32[32,640]{1,0:T(8,128)}, u32[]{:S(2)}) copy-start(s32[32,640]{1,0:T(8,128)} %band.1) | copy-start | bytes 245764
  4.0 13.1 %copy-start.6 = (s32[32]{0:T(128)S(1)}, s32[32]{0:T(128)}, u32[]{:S(2)}) copy-start(s32[32]{0:T(128)} %tally.1) | copy-start | bytes 388
  4.0 13.1 %copy-start.7 = (s32[16]{0:T(128)S(1)}, s32[16]{0:T(128)}, u32[]{:S(2)}) copy-start(s32[16]{0:T(128)} %taper.1) | copy-start | bytes 196
  4.0 13.1 %copy-start.8 = (s32[64]{0:T(128)S(1)}, s32[64]{0:T(128)}, u32[]{:S(2)}) copy-start(s32[64]{0:T(128)} %constant.27.clone.hosted) | copy-start | bytes 772
  4.1 32.3 %all-to-all-start = ((bf16[32,32,384]{2,1,0:T(8,128)(2,1)}), bf16[32,32,384]{2,1,0:T(8,128)(2,1)S(1)}, u32[]{:S(2)}, u32[]{:S(2)}) async-start(bf16[32,32,384]{2,1,0:T(8,128)(2,1)} %entry.1), calls=%async_computation | async-start | bytes 1572864 | tf_op jit(solution)/shard_map/all_to_all | solution.py:329
  37.0 13.1 %collective-permute-start = (bf16[192,1024]{1,0:T(8,128)(2,1)S(1)}, bf16[192,1024]{1,0:T(8,128)(2,1)S(1)}, u32[]{:S(2)}, u32[]{:S(2)}) collective-permute-start(bf16[192,1024]{1,0:T(8,128)(2,1)S(1)} %get-tuple-element.18), channel_id=1, source_target_pairs={{0,128},{128,144},{144,272},{272,256},{256,368},{368,352},{352,224... | collective-permute-start | bytes 1179656 | tf_op jit(solution)/shard_map/ppermute | solution.py:339
  42.3 8.8 %collective-permute-start.1 = (bf16[192,1024]{1,0:T(8,128)(2,1)S(1)}, bf16[192,1024]{1,0:T(8,128)(2,1)S(1)}, u32[]{:S(2)}, u32[]{:S(2)}) collective-permute-start(bf16[192,1024]{1,0:T(8,128)(2,1)S(1)} %get-tuple-element.19), channel_id=1, source_target_pairs={{128,0},{144,128},{272,144},{256,272},{368,256},{352,368},{224,352... | collective-permute-start | bytes 1179656 | tf_op jit(solution)/shard_map/ppermute | solution.py:340
where the time goes:
time: 93.2 us; the launch traced here: 92.9 us
  blocking collectives  33.3 us (36%)
  starting transfers between devices  22.3 us (24%)
  waiting for transfers between devices  21.8 us (23%)
  Pallas kernels  13.5 us (14%)
  local copies, waits for them, and re-layouts  1.8 us (2%)
    all_to_all x1, blocking collectives, local(): lax.all_to_all(analysed, 'member', split_axis=0, concat_axis=0, tiled=True)  33.3 us
    all_to_all x1, waiting for transfers between devices, local(): lax.all_to_all(sent, 'member', split_axis=0, concat_axis=0, tiled=True)  17.9 us
    all_to_all x1, starting transfers between devices, local(): lax.all_to_all(sent, 'member', split_axis=0, concat_axis=0, tiled=True)  13 us
    pallas_call x1, Pallas kernels, analyse(): call(analyse_kernel, 'analyse', 0, 11, shape(ROWS, CORE), [pltpu.VMEM((CO...  6.31 us
    ppermute x1, starting transfers between devices, local(): before = lax.ppermute(rightward, axes, up)  5.36 us
    ppermute x1, starting transfers between devices, local(): after = lax.ppermute(leftward, axes, down)  3.95 us
    ppermute x1, waiting for transfers between devices, local(): before = lax.ppermute(rightward, axes, up)  2.86 us
    pallas_call x1, Pallas kernels, enter(): call(entry_kernel, 'entry', 2, 1, shape(GROUP, PADDED, CORE), flops=4 * 5...  2.16 us
  transfers between devices with their start and end apart: 3, of which 3 were waited for; matrix products, arithmetic and copies ran while one was open for 0% of the time, Pallas kernels for 2%

commit v1 on v0

--- a/solution.py
+++ b/solution.py
@@ -19,7 +19,7 @@
 PADDED = 32
 ROWS = GROUP * PADDED
 MEMBERS = GROUP * HELD
-HALF = 16
+EIGHT = 8
 TILE = 256
 
 F32 = jnp.float32
@@ -32,7 +32,6 @@
     (0, 1, 9, 10, 2, 26, 27, 3, 11, 12, 13, 14, 6, 30, 22, 21,
      29, 5, 4, 28, 20, 19, 18, 17, 25, 24, 16, 8, 15, 23, 31, 7),
 )
-HOMES = np.array(CYCLES, np.int32).reshape(-1)
 HOSTED = np.argsort(np.array(CYCLES, np.int32), axis=1).astype(np.int32).reshape(-1)
 
 
@@ -44,6 +43,10 @@
     return pl.BlockSpec(memory_space=pltpu.SMEM)
 
 
+def hbm():
+    return pl.BlockSpec(memory_space=pltpu.HBM)
+
+
 def params():
     return pltpu.CompilerParams(vmem_limit_bytes=40 * 1024 * 1024)
 
@@ -60,41 +63,66 @@
     return lax.dot_general(a, b, (((1,), (1,)), ((), ())), preferred_element_type=F32)
 
 
-def swap_matrix(rows, columns, inner):
-    row = lax.broadcasted_iota(I32, (rows, columns), 0)
-    column = lax.broadcasted_iota(I32, (rows, columns), 1)
-    outer = rows // inner
-    wanted = (row & (inner - 1)) * outer + row // inner
+def swap_matrix(inner):
+    size = GROUP * EIGHT
+    row = lax.broadcasted_iota(I32, (size, size), 0)
+    column = lax.broadcasted_iota(I32, (size, size), 1)
+    wanted = (row & (inner - 1)) * (size // inner) + row // inner
     return jnp.where(column == wanted, 1.0, 0.0).astype(BF16)
 
 
-def entry_kernel(place, homes, states, out):
-    first = place[0] * GROUP
-    swap = swap_matrix(GROUP * HALF, GROUP * HALF, HALF)
-    for start in (0, HALF):
-        count = min(HALF, HELD - start)
-        block = states[start : start + count].reshape(count * GROUP, CORE)
-        moved = mm(swap[:, : count * GROUP], block).astype(BF16)
+def core_index():
+    return lax.axis_index("patch") % 2
+
+
+def home_of(core, patch):
+    return jnp.where(core == 0, CYCLES[0][patch], CYCLES[1][patch])
+
+
+def entry_kernel(states, out):
+    swap = swap_matrix(EIGHT)
+    core = core_index()
+    for start in range(0, HELD, 2 * EIGHT):
+        halves = []
+        for first in (start, start + EIGHT):
+            count = min(EIGHT, HELD - first)
+            block = states[first : first + count].reshape(count * GROUP, CORE)
+            halves.append(mm(swap[:, : count * GROUP], block))
         for p in range(GROUP):
-            out[homes[first + p], start : start + HALF, :] = moved[p * HALF : (p + 1) * HALF, :]
-
-
-def exit_kernel(place, homes, analysed, out, ordered):
-    first = place[0] * GROUP
-    swap = swap_matrix(GROUP * HALF, GROUP * HALF, GROUP)
-    for start in (0, HALF):
-        count = min(HALF, HELD - start)
-        for p in range(GROUP):
-            ordered[p * HALF : (p + 1) * HALF, :] = analysed[homes[first + p], start : start + HALF, :]
-        moved = mm(swap[: count * GROUP, :], ordered[...]).astype(BF16)
-        out[start : start + count] = moved.reshape(count, GROUP, CORE)
+            rows = slice(p * EIGHT, (p + 1) * EIGHT)
+            both = jnp.concatenate([half[rows, :] for half in halves], axis=0)
+            out[home_of(core, p), start : start + 2 * EIGHT, :] = both.astype(BF16)
+
+
+def exit_kernel(analysed, out, buffer, sent):
+    swap = swap_matrix(GROUP)
+    core = core_index()
+    copies = []
+    for start in range(0, HELD, 2 * EIGHT):
+        tiles = [
+            analysed[home_of(core, p), start : start + 2 * EIGHT, :].astype(F32)
+            for p in range(GROUP)
+        ]
+        for k in range(2):
+            first = start + k * EIGHT
+            count = min(EIGHT, HELD - first)
+            block = jnp.concatenate([tile[k * EIGHT : (k + 1) * EIGHT, :] for tile in tiles], axis=0)
+            moved = mm(swap[: count * GROUP, :], block.astype(BF16)).astype(BF16)
+            buffer[first : first + count] = moved.reshape(count, GROUP, CORE)
+        rows = slice(start, min(start + 2 * EIGHT, HELD))
+        copies.append(
+            pltpu.make_async_copy(buffer.at[rows], out.at[rows], sent.at[start // (2 * EIGHT)])
+        )
+        copies[-1].start()
+    for copy in copies:
+        copy.wait()
 
 
 def prepare_kernel(
-    place, hosted, tally, taper, location, datum, error_spread, band,
+    hosted, tally, taper, location, datum, error_spread, band,
     root_column, ratio_column, root_row, pick,
 ):
-    me = hosted[place[0] * GROUP + place[1]]
+    me = hosted[core_index() * GROUP + lax.axis_index("member")]
     mine = pl.ds(me, 1)
     flat = location[mine, :]
     level = flat >> 5
@@ -175,36 +203,38 @@
 def analyse_kernel(
     before, after, spread, state_mean, own_gram, own_basis, own_pulls, sums,
     root_column, ratio_column, root_row,
-    out, fringe_t, fringe, gram, basis, pulls,
+    out, fringe_t, fringe, gram, basis, pulls, first, second, third, fourth,
 ):
     live = (lax.broadcasted_iota(I32, (RIM, ROWS), 1) & (PADDED - 1)) < HELD
     for rims, top in ((before, 0), (after, RIM)):
         rows = slice(top, top + RIM)
         tile = rims[...].astype(F32)
         mean = jnp.sum(tile, axis=1, keepdims=True) / MEMBERS
-        tile = jnp.where(live, tile - mean, 0.0)
-        fringe_t[rows, :] = tile.astype(BF16)
-        fringe[:, rows] = tile.T.astype(BF16)
+        fringe_t[rows, :] = jnp.where(live, tile - mean, 0.0).astype(BF16)
         span = slice(CORE + top, CORE + top + RIM)
         pulls[span, :] = ratio_column[span, :] - root_column[span, :] * mean
     pulls[:CORE, :] = own_pulls[...]
     gram[:CORE, :CORE] = own_gram[...]
     basis[:CORE, :] = own_basis[...]
-
+    first[:CORE, :CORE] = own_basis[...].astype(BF16)
+    first[:, CORE:] = pulls[...].astype(BF16)
+
+    corner = lax.broadcasted_iota(I32, (128, 128), 0) == lax.broadcasted_iota(I32, (128, 128), 1)
     squares = sums[0:1, 0:1]
     trace = sums[8:9, 0:1]
-    corner = lax.broadcasted_iota(I32, (128, 128), 0) == lax.broadcasted_iota(I32, (128, 128), 1)
     for t in range(0, CORE, 128):
-        root = root_column[CORE + t : CORE + t + 128, :]
-        root = jnp.tile(root, (1, CORE // 128))
-        lifted = root * mm(fringe_t[t : t + 128, :], spread[...])
-        basis[CORE + t : CORE + t + 128, :] = lifted
+        rows = slice(CORE + t, CORE + t + 128)
+        root = jnp.tile(root_column[rows, :], (1, CORE // 128))
+        strip = fringe_t[t : t + 128, :]
+        lifted = root * mm(strip, spread[...])
+        basis[rows, :] = lifted
+        first[rows, :CORE] = lifted.astype(BF16)
         block = lifted * root_row[0:1, :CORE]
-        gram[CORE + t : CORE + t + 128, :CORE] = block.astype(BF16)
-        gram[:CORE, CORE + t : CORE + t + 128] = block.T.astype(BF16)
+        gram[rows, :CORE] = block.astype(BF16)
+        gram[:CORE, rows] = block.astype(BF16).T
         squares += 2.0 * jnp.sum(block * block, keepdims=True)
-        block = root * mm(fringe_t[t : t + 128, :], fringe[...]) * root_row[0:1, CORE:]
-        gram[CORE + t : CORE + t + 128, CORE:] = block.astype(BF16)
+        block = root * mm_nt(strip, fringe_t[...]) * root_row[0:1, CORE:]
+        gram[rows, CORE:] = block.astype(BF16)
         squares += jnp.sum(block * block, keepdims=True)
         trace += jnp.sum(jnp.where(corner, block[:, t : t + 128], 0.0), keepdims=True)
     draw = F32(MEMBERS - 1)
@@ -213,45 +243,57 @@
     a = draw * inverse
     r = 1.5 - 0.5 * a
     s = 1.5 - 0.5 * a * r * r
-    z = basis[...] * inverse
-    d = pulls[...]
-
-    def step(*parts):
-        both = jnp.concatenate(parts, axis=1).astype(BF16)
-        product = mm(gram[...], both) * inverse
+
+    def step(source):
+        product = mm(gram[...], source[...])
         return product[:, :CORE], product[:, CORE:]
 
-    v = -0.5 * z
-    pv, px = step(v, d)
-    v = 2.0 * r * v - 0.5 * pv
-    x = r * d - 0.5 * px
-    pv, px = step(v, x)
-    v = -0.5 * (r * r * z + a * v + pv)
-    x = r * x - 0.5 * px
-    pv, px = step(v, x)
-    v = r * v - 0.5 * s * z - 0.5 * pv
-    x = 1.5 * d - 0.5 * (a * x + px)
-    x = r * x - 0.5 * inverse * mm(gram[...], x.astype(BF16))
-    y = inverse * mm(gram[...], x.astype(BF16))
+    def turn(t):
+        fringe[:, t : t + 128] = fringe_t[t : t + 128, :].T
+
+    turn(0)
+    pv, px = step(first)
+    v = (0.25 * inverse * inverse) * pv - (r * inverse) * basis[...]
+    second[:, :CORE] = v.astype(BF16)
+    second[:, CORE:] = (r * pulls[...] - (0.5 * inverse) * px).astype(BF16)
+
+    turn(128)
+    pv, px = step(second)
+    v = (0.5 * a) * second[:, :CORE].astype(F32) + (0.5 * inverse) * pv
+    v += (0.5 * r * r * inverse) * basis[...]
+    third[:, :CORE] = (-v).astype(BF16)
+    x = r * second[:, CORE:].astype(F32) - (0.5 * inverse) * px
+    third[:, CORE:] = x.astype(BF16)
+
+    turn(256)
+    pv, px = step(third)
+    v = r * third[:, :CORE].astype(F32) - (0.5 * inverse) * pv
+    v -= (0.5 * s * inverse) * basis[...]
+    fourth[:, :CORE] = v.astype(BF16)
+    x = (0.5 * a) * third[:, CORE:].astype(F32) + (0.5 * inverse) * px
+    fourth[:, CORE:] = (1.5 * pulls[...] - x).astype(BF16)
+    first[:, :CORE] = (jnp.tile(root_column[...], (1, CORE // 128)) * v).astype(BF16)
+
+    pv, px = step(fourth)
+    x = inverse * (r * fourth[:, CORE:].astype(F32) - (0.5 * inverse) * px)
     shift = []
     for t in range(0, CORE, 128):
-        both = r * s * x * z[:, t : t + 128] + y * v[:, t : t + 128]
-        shift.append(jnp.sum(both, axis=0, keepdims=True))
+        both = (r * s) * basis[:, t : t + 128] + pv[:, t : t + 128]
+        shift.append(jnp.sum(x * both, axis=0, keepdims=True))
     base = state_mean[0:1, :] + jnp.concatenate(shift, axis=1)
-    lift = (jnp.tile(root_column[...], (1, CORE // 128)) * v).astype(BF16)
     gain = jnp.sqrt(a)
     for t in range(0, ROWS, TILE):
         own = spread[t : t + TILE, :]
-        moved = mm(own, lift[:CORE, :]) + mm(fringe[t : t + TILE, :], lift[CORE:, :])
+        moved = mm(own, first[:CORE, :CORE]) + mm(fringe[t : t + TILE, :], first[CORE:, :CORE])
         moved += r * s * own.astype(F32)
         out[t : t + TILE, :] = (base + gain * moved).astype(BF16)
 
 
-def call(kernel, name, smems, vmems, out_shape, scratch_shapes=(), flops=0):
+def call(kernel, name, in_specs, out_shape, out_specs=None, scratch_shapes=(), flops=0):
     return pl.pallas_call(
         kernel,
-        in_specs=[smem()] * smems + [vmem()] * vmems,
-        out_specs=jax.tree.map(lambda _: vmem(), out_shape),
+        in_specs=in_specs,
+        out_specs=out_specs or jax.tree.map(lambda _: vmem(), out_shape),
         out_shape=out_shape,
         scratch_shapes=list(scratch_shapes),
         compiler_params=params(),
@@ -260,38 +302,39 @@
     )
 
 
-def enter(place, homes, states):
-    return call(
-        entry_kernel, "entry", 2, 1, shape(GROUP, PADDED, CORE), flops=4 * 512 * 512 * CORE
-    )(place, homes, states)
-
-
-def leave(place, homes, analysed):
-    return call(
-        exit_kernel, "exit", 2, 1, shape(HELD, GROUP, CORE),
-        [pltpu.VMEM((GROUP * HALF, CORE), BF16)], 4 * 512 * 512 * CORE,
-    )(place, homes, analysed)
-
-
-def prepare(place, hosted, tally, taper, location, datum, error_spread, band):
-    return call(
-        prepare_kernel, "prepare", 4, 4,
+def enter(states):
+    return call(
+        entry_kernel, "entry", [vmem()], shape(GROUP, PADDED, CORE), flops=8 * 256 * 256 * CORE
+    )(states)
+
+
+def leave(analysed):
+    return call(
+        exit_kernel, "exit", [vmem()], shape(HELD, GROUP, CORE), hbm(),
+        [pltpu.VMEM((HELD, GROUP, CORE), BF16), pltpu.SemaphoreType.DMA((2,))],
+        8 * 256 * 256 * CORE,
+    )(analysed)
+
+
+def prepare(hosted, tally, taper, location, datum, error_spread, band):
+    return call(
+        prepare_kernel, "prepare", [smem()] * 3 + [vmem()] * 4,
         [shape(SPAN, 128, dtype=F32), shape(SPAN, 128, dtype=F32), shape(8, SPAN, dtype=F32),
          shape(2 * RIM, CORE)],
         flops=4 * SPAN * OBS,
-    )(place, hosted, tally, taper, location, datum, error_spread, band)
+    )(hosted, tally, taper, location, datum, error_spread, band)
 
 
 def extract(states, pick):
     return call(
-        extract_kernel, "extract", 0, 2, [shape(RIM, ROWS), shape(RIM, ROWS)],
+        extract_kernel, "extract", [vmem()] * 2, [shape(RIM, ROWS), shape(RIM, ROWS)],
         flops=4 * RIM * CORE * ROWS,
     )(states, pick)
 
 
 def own_part(states, root_column, ratio_column, root_row):
     return call(
-        own_kernel, "own_part", 0, 4,
+        own_kernel, "own_part", [vmem()] * 4,
         [shape(ROWS, CORE), shape(8, CORE, dtype=F32), shape(CORE, CORE),
          shape(CORE, CORE, dtype=F32), shape(CORE, 128, dtype=F32), shape(16, 128, dtype=F32)],
         flops=2 * ROWS * CORE * CORE,
@@ -299,16 +342,18 @@
 
 
 def analyse(before, after, own, prepared):
-    return call(
-        analyse_kernel, "analyse", 0, 11, shape(ROWS, CORE),
-        [
+    chain = pltpu.VMEM((SPAN, CORE + 128), BF16)
+    return call(
+        analyse_kernel, "analyse", [vmem()] * 11, shape(ROWS, CORE),
+        scratch_shapes=[
             pltpu.VMEM((CORE, ROWS), BF16),
             pltpu.VMEM((ROWS, CORE), BF16),
             pltpu.VMEM((SPAN, SPAN), BF16),
             pltpu.VMEM((SPAN, CORE), F32),
             pltpu.VMEM((SPAN, 128), F32),
+            chain, chain, chain, chain,
         ],
-        8 * SPAN * SPAN * CORE,
+        flops=8 * SPAN * SPAN * CORE,
     )(before, after, *own, *prepared)
 
 
@@ -323,13 +368,11 @@
 ):
     axes = ("member", "patch")
     groups = lax.axis_size("patch")
-    place = jnp.stack([lax.axis_index("patch") % 2, lax.axis_index("member")]).astype(I32)
-    homes = jnp.asarray(HOMES)
-    sent = enter(place, homes, jnp.transpose(background_fields, (1, 0, 2)))
+    sent = enter(jnp.transpose(background_fields, (1, 0, 2)))
     received = lax.all_to_all(sent, "member", split_axis=0, concat_axis=0, tiled=True)
     *prepared, pick = prepare(
-        place, jnp.asarray(HOSTED), measured_tally, taper_weights, measured_location,
-        measured_datum, measured_error_spread, measured_distance_band,
+        jnp.asarray(HOSTED), measured_tally, taper_weights, measured_location, measured_datum,
+        measured_error_spread, measured_distance_band,
     )
     states = received.reshape(ROWS, CORE)
     rightward, leftward = extract(states, pick)
@@ -341,7 +384,7 @@
     own = own_part(states, *prepared)
     analysed = analyse(before, after, own, prepared).reshape(GROUP, PADDED, CORE)
     returned = lax.all_to_all(analysed, "member", split_axis=0, concat_axis=0, tiled=True)
-    return jnp.transpose(leave(place, homes, returned), (1, 0, 2))
+    return jnp.transpose(leave(returned), (1, 0, 2))
 
 
 def solution(mesh):

time: 93.2 us -> 89.7 us (0.962)
  Pallas kernels: 13.5 us -> 10.7 us
    pallas_call x6, Pallas kernels: 13.5 us -> 10.7 us  [the longest x1 5.26 us: analyse(): call(analyse_kernel, 'analyse', [vmem()] * 11, shape(ROWS, CORE), scratch...]
  transfers between devices with their start and end apart: 3 -> 3, of which waited for: 3 -> 3; matrix products, arithmetic and copies ran while one was open for 0% -> 0% of each run, Pallas kernels for 2% -> 3%
where the time goes in v1:
time: 89.7 us; the launch traced here: 89.3 us
  blocking collectives  33.3 us (37%)
  starting transfers between devices  22.3 us (25%)
  waiting for transfers between devices  21.8 us (24%)
  Pallas kernels  10.7 us (12%)
  local copies, waits for them, and re-layouts  1.15 us (1%)
    all_to_all x1, blocking collectives, local(): lax.all_to_all(analysed, 'member', split_axis=0, concat_axis=0, tiled=True)  33.3 us
    all_to_all x1, waiting for transfers between devices, local(): lax.all_to_all(sent, 'member', split_axis=0, concat_axis=0, tiled=True)  17.9 us
    all_to_all x1, starting transfers between devices, local(): lax.all_to_all(sent, 'member', split_axis=0, concat_axis=0, tiled=True)  13 us
    ppermute x1, starting transfers between devices, local(): before = lax.ppermute(rightward, axes, up)  5.36 us
    pallas_call x1, Pallas kernels, analyse(): call(analyse_kernel, 'analyse', [vmem()] * 11, shape(ROWS, CORE), scratch...  5.26 us
    ppermute x1, starting transfers between devices, local(): after = lax.ppermute(leftward, axes, down)  3.94 us
    ppermute x1, waiting for transfers between devices, local(): before = lax.ppermute(rightward, axes, up)  2.86 us
  transfers between devices with their start and end apart: 3, of which 3 were waited for; matrix products, arithmetic and copies ran while one was open for 0% of the time, Pallas kernels for 3%

profile of v1, /device:TPU:25, one launch (start us, length us, event | category | flops | bytes accessed | tf_op | source)
XLA Modules:
  0.0 89.3 jit_solution(3292159183118771541)
XLA Ops:
  0.0 0.0 copy-start
  0.0 1.1 %copy-done = bf16[32,30,384]{2,0,1:T(8,128)(2,1)S(1)} copy-done((bf16[32,30,384]{2,0,1:T(8,128)(2,1)S(1)}, bf16[32,30,384]{2,0,1:T(8,128)(2,1)}, u32[]{:S(2)}) %copy-start) | copy-done | bytes 737304
  1.1 1.3 %entry.1 = bf16[32,32,384]{2,1,0:T(8,128)(2,1)} custom-call(bf16[30,32,384]{2,1,0:T(8,128)(2,1)S(1)} %bitcast.7), custom_call_target="tpu_custom_call" | custom-call | flops 201326592 | bytes 1048576 | tf_op jit(solution)/shard_map/entry/pallas_call | solution.py:306
  2.5 0.0 copy-start.1
  2.5 0.0 copy-start.2
  2.5 0.0 copy-start.3
  2.5 0.0 copy-start.4
  2.5 0.0 copy-start.5
  2.5 0.0 copy-start.6
  2.5 0.0 copy-start.7
  2.5 13.0 %all-to-all-start = ((bf16[32,32,384]{2,1,0:T(8,128)(2,1)}), bf16[32,32,384]{2,1,0:T(8,128)(2,1)S(1)}, u32[]{:S(2)}, u32[]{:S(2)}) async-start(bf16[32,32,384]{2,1,0:T(8,128)(2,1)} %entry.1), calls=%async_computation | async-start | bytes 1572864 | tf_op jit(solution)/shard_map/all_to_all | solution.py:372
  15.5 0.0 copy-done.1
  15.6 0.0 copy-done.2
  15.6 0.0 copy-done.3
  15.6 0.0 copy-done.4
  15.6 0.0 copy-done.5
  15.6 0.0 copy-done.6
  15.6 0.0 copy-done.7
  15.6 1.3 %prepare.1 = (f32[768,128]{1,0:T(8,128)S(1)}, f32[768,128]{1,0:T(8,128)S(1)}, f32[8,768]{1,0:T(8,128)S(1)}, bf16[384,384]{1,0:T(8,128)(2,1)S(1)}) custom-call(s32[64]{0:T(128)S(1)} %copy-done.7, s32[32]{0:T(128)S(1)} %copy-done.5, s32[16]{0:T(128)S(1)} %copy-done.6, s32[32,640]{1,0:T(8,128)S(1)} %copy-done.1, f32[32,640]{1,0:T(8,128)S(1)} %copy-done.2, ...), custom_call_target="tpu_custom_call" | custom-call | flops 1966080 | bytes 1048576 | tf_op jit(solution)/shard_map/prepare/pallas_call | solution.py:320
  16.9 17.9 %all-to-all-done = bf16[32,32,384]{2,1,0:T(8,128)(2,1)S(1)} async-done(((bf16[32,32,384]{2,1,0:T(8,128)(2,1)}), bf16[32,32,384]{2,1,0:T(8,128)(2,1)S(1)}, u32[]{:S(2)}, u32[]{:S(2)}) %all-to-all-start) | async-done | bytes 786464 | tf_op jit(solution)/shard_map/all_to_all | solution.py:372
  34.8 0.6 extract.1
  35.4 5.4 %collective-permute-start = (bf16[192,1024]{1,0:T(8,128)(2,1)S(1)}, bf16[192,1024]{1,0:T(8,128)(2,1)S(1)}, u32[]{:S(2)}, u32[]{:S(2)}) collective-permute-start(bf16[192,1024]{1,0:T(8,128)(2,1)S(1)} %get-tuple-element.18), channel_id=1, source_target_pairs={{0,128},{128,144},{144,272},{272,256},{256,368},{368,352},{352,224... | collective-permute-start | bytes 1179656 | tf_op jit(solution)/shard_map/ppermute | solution.py:382
  40.8 3.9 %collective-permute-start.1 = (bf16[192,1024]{1,0:T(8,128)(2,1)S(1)}, bf16[192,1024]{1,0:T(8,128)(2,1)S(1)}, u32[]{:S(2)}, u32[]{:S(2)}) collective-permute-start(bf16[192,1024]{1,0:T(8,128)(2,1)S(1)} %get-tuple-element.19), channel_id=1, source_target_pairs={{128,0},{144,128},{272,144},{256,272},{368,256},{352,368},{224,352... | collective-permute-start | bytes 1179656 | tf_op jit(solution)/shard_map/ppermute | solution.py:383
  44.7 0.9 %own_part.1 = (bf16[1024,384]{1,0:T(8,128)(2,1)S(1)}, f32[8,384]{1,0:T(8,128)S(1)}, bf16[384,384]{1,0:T(8,128)(2,1)S(1)}, f32[384,384]{1,0:T(8,128)S(1)}, f32[384,128]{1,0:T(8,128)S(1)}, /*index=5*/f32[16,128]{1,0:T(8,128)S(1)}) custom-call(bf16[1024,384]{1,0:T(8,128)(2,1)S(1)} %bitcast.5, f32[768,128]{1,0:T(8,128)S(1)} %get-tuple-element.20.root_column, ...), custom_call_target="tpu_custom_call" | custom-call | flops 301989888 | bytes 1048576 | tf_op jit(solution)/shard_map/own_part/pallas_call | solution.py:336
  45.7 2.9 %collective-permute-done.before = bf16[192,1024]{1,0:T(8,128)(2,1)S(1)} collective-permute-done((bf16[192,1024]{1,0:T(8,128)(2,1)S(1)}, bf16[192,1024]{1,0:T(8,128)(2,1)S(1)}, u32[]{:S(2)}, u32[]{:S(2)}) %collective-permute-start) | collective-permute-done | bytes 393248 | tf_op jit(solution)/shard_map/ppermute | solution.py:382
  48.5 1.1 %collective-permute-done.1.after = bf16[192,1024]{1,0:T(8,128)(2,1)S(1)} collective-permute-done((bf16[192,1024]{1,0:T(8,128)(2,1)S(1)}, bf16[192,1024]{1,0:T(8,128)(2,1)S(1)}, u32[]{:S(2)}, u32[]{:S(2)}) %collective-permute-start.1) | collective-permute-done | bytes 393248 | tf_op jit(solution)/shard_map/ppermute | solution.py:383
  49.6 5.3 %analyse.1 = bf16[1024,384]{1,0:T(8,128)(2,1)S(1)} custom-call(bf16[192,1024]{1,0:T(8,128)(2,1)S(1)} %collective-permute-done.before, bf16[192,1024]{1,0:T(8,128)(2,1)S(1)} %collective-permute-done.1.after, bf16[1024,384]{1,0:T(8,128)(2,1)S(1)} %get-tuple-element.23.spread, f32[8,384]{1,0:T(8,128)S(1)} %get-tuple-element.24.state_mean, ...), custom_call_target="tpu_custom_call" | custom-call | flops 1811939328 | bytes 1048576 | tf_op jit(solution)/shard_map/analyse/pallas_call | solution.py:346
  54.9 33.3 %all_to_all.10.analysed = bf16[32,32,384]{2,1,0:T(8,128)(2,1)S(1)} all-to-all(bf16[32,32,384]{2,1,0:T(8,128)(2,1)S(1)} %bitcast.6), channel_id=1, replica_groups=mesh['member'=32,'patch'=16] {'member'}, dimensions={0} | all-to-all | bytes 1572864 | tf_op jit(solution)/shard_map/all_to_all | solution.py:386
  88.1 1.2 %exit.1 = bf16[30,32,384]{2,1,0:T(8,128)(2,1)} custom-call(bf16[32,32,384]{2,1,0:T(8,128)(2,1)S(1)} %all_to_all.10.analysed), custom_call_target="tpu_custom_call" | custom-call | flops 201326592 | bytes 1048576 | tf_op jit(solution)/shard_map/exit/pallas_call | solution.py:312
Async XLA Ops:
  0.0 1.1 %copy-start = (bf16[32,30,384]{2,0,1:T(8,128)(2,1)S(1)}, bf16[32,30,384]{2,0,1:T(8,128)(2,1)}, u32[]{:S(2)}) copy-start(bf16[32,30,384]{2,0,1:T(8,128)(2,1)} %param.8) | copy-start | bytes 2211844
  2.5 13.1 %copy-start.1 = (s32[32,640]{1,0:T(8,128)S(1)}, s32[32,640]{1,0:T(8,128)}, u32[]{:S(2)}) copy-start(s32[32,640]{1,0:T(8,128)} %location.1) | copy-start | bytes 245764
  2.5 13.1 %copy-start.2 = (f32[32,640]{1,0:T(8,128)S(1)}, f32[32,640]{1,0:T(8,128)}, u32[]{:S(2)}) copy-start(f32[32,640]{1,0:T(8,128)} %datum.1) | copy-start | bytes 245764
  2.5 13.1 %copy-start.3 = (f32[32,640]{1,0:T(8,128)S(1)}, f32[32,640]{1,0:T(8,128)}, u32[]{:S(2)}) copy-start(f32[32,640]{1,0:T(8,128)} %error_spread.1) | copy-start | bytes 245764
  2.5 13.1 %copy-start.4 = (s32[32,640]{1,0:T(8,128)S(1)}, s32[32,640]{1,0:T(8,128)}, u32[]{:S(2)}) copy-start(s32[32,640]{1,0:T(8,128)} %band.1) | copy-start | bytes 245764
  2.5 13.1 %copy-start.5 = (s32[32]{0:T(128)S(1)}, s32[32]{0:T(128)}, u32[]{:S(2)}) copy-start(s32[32]{0:T(128)} %tally.1) | copy-start | bytes 388
  2.5 13.1 %copy-start.6 = (s32[16]{0:T(128)S(1)}, s32[16]{0:T(128)}, u32[]{:S(2)}) copy-start(s32[16]{0:T(128)} %taper.1) | copy-start | bytes 196
  2.5 13.1 %copy-start.7 = (s32[64]{0:T(128)S(1)}, s32[64]{0:T(128)}, u32[]{:S(2)}) copy-start(s32[64]{0:T(128)} %constant.2.clone.hosted) | copy-start | bytes 772
  2.5 32.3 %all-to-all-start = ((bf16[32,32,384]{2,1,0:T(8,128)(2,1)}), bf16[32,32,384]{2,1,0:T(8,128)(2,1)S(1)}, u32[]{:S(2)}, u32[]{:S(2)}) async-start(bf16[32,32,384]{2,1,0:T(8,128)(2,1)} %entry.1), calls=%async_computation | async-start | bytes 1572864 | tf_op jit(solution)/shard_map/all_to_all | solution.py:372
  35.4 13.1 %collective-permute-start = (bf16[192,1024]{1,0:T(8,128)(2,1)S(1)}, bf16[192,1024]{1,0:T(8,128)(2,1)S(1)}, u32[]{:S(2)}, u32[]{:S(2)}) collective-permute-start(bf16[192,1024]{1,0:T(8,128)(2,1)S(1)} %get-tuple-element.18), channel_id=1, source_target_pairs={{0,128},{128,144},{144,272},{272,256},{256,368},{368,352},{352,224... | collective-permute-start | bytes 1179656 | tf_op jit(solution)/shard_map/ppermute | solution.py:382
  40.8 8.8 %collective-permute-start.1 = (bf16[192,1024]{1,0:T(8,128)(2,1)S(1)}, bf16[192,1024]{1,0:T(8,128)(2,1)S(1)}, u32[]{:S(2)}, u32[]{:S(2)}) collective-permute-start(bf16[192,1024]{1,0:T(8,128)(2,1)S(1)} %get-tuple-element.19), channel_id=1, source_target_pairs={{128,0},{144,128},{272,144},{256,272},{368,256},{352,368},{224,352... | collective-permute-start | bytes 1179656 | tf_op jit(solution)/shard_map/ppermute | solution.py:383

commit v2 on v1

--- a/solution.py
+++ b/solution.py
@@ -168,9 +168,18 @@
         leftward[:, t : t + TILE] = rims[RIM:, :]
 
 
+def corners(block):
+    same = lax.broadcasted_iota(I32, block.shape, 0) == lax.broadcasted_iota(I32, block.shape, 1)
+    return jnp.sum(jnp.where(same, block, 0.0), keepdims=True)
+
+
+def squared(block):
+    return jnp.sum(block * block, keepdims=True)
+
+
 def own_kernel(
     states, root_column, ratio_column, root_row,
-    spread, state_mean, gram, basis, pulls, sums,
+    window, gram, basis, first, pulls, state_mean, sums,
 ):
     total = jnp.zeros((1, CORE), F32)
     for t in range(0, ROWS, TILE):
@@ -181,121 +190,144 @@
     covariance = jnp.zeros((CORE, CORE), F32)
     for t in range(0, ROWS, TILE):
         tile = jnp.where(live, states[t : t + TILE, :].astype(F32) - mean, 0.0)
-        spread[t : t + TILE, :] = tile.astype(BF16)
+        window[t : t + TILE, :CORE] = tile.astype(BF16)
         covariance += mm(tile.T.astype(BF16), tile.astype(BF16))
-    squares = jnp.zeros((1, 1), F32)
-    trace = jnp.zeros((1, 1), F32)
-    corner = lax.broadcasted_iota(I32, (128, 128), 0) == lax.broadcasted_iota(I32, (128, 128), 1)
-    column_mean = jnp.broadcast_to(mean, (128, CORE)).T
-    for t in range(0, CORE, 128):
-        root = root_column[t : t + 128, :]
-        lifted = jnp.tile(root, (1, CORE // 128)) * covariance[t : t + 128, :]
-        basis[t : t + 128, :] = lifted
-        block = lifted * root_row[0:1, :CORE]
-        gram[t : t + 128, :] = block.astype(BF16)
-        squares += jnp.sum(block * block, keepdims=True)
-        trace += jnp.sum(jnp.where(corner, block[:, t : t + 128], 0.0), keepdims=True)
-        pulls[t : t + 128, :] = ratio_column[t : t + 128, :] - root * column_mean[t : t + 128, :]
-    sums[0:8, :] = jnp.broadcast_to(squares, (8, 128))
-    sums[8:16, :] = jnp.broadcast_to(trace, (8, 128))
+    root = root_column[:CORE, :]
+    lifted = jnp.tile(root, (1, CORE // 128)) * covariance
+    basis[:CORE, :] = lifted
+    first[:CORE, :CORE] = lifted.astype(BF16)
+    block = lifted * root_row[0:1, :CORE]
+    gram[:CORE, :CORE] = block.astype(BF16)
+    pull = ratio_column[:CORE, :] - root * jnp.broadcast_to(mean, (128, CORE)).T
+    pulls[:CORE, :] = pull
+    first[:CORE, CORE:] = pull.astype(BF16)
+    sums[0:8, :] = jnp.broadcast_to(squared(block), (8, 128))
+    sums[8:16, :] = jnp.broadcast_to(corners(block), (8, 128))
+
+
+def add_rim(rims, top, earlier, root_column, ratio_column, root_row, window, gram, basis, first, pulls):
+    span = slice(top, top + RIM)
+    live = (lax.broadcasted_iota(I32, (RIM, ROWS), 1) & (PADDED - 1)) < HELD
+    tile = rims[...].astype(F32)
+    mean = jnp.sum(tile, axis=1, keepdims=True) / MEMBERS
+    strip = jnp.where(live, tile - mean, 0.0).astype(BF16)
+    narrow = root_column[span, :]
+    pull = ratio_column[span, :] - narrow * mean
+    pulls[span, :] = pull
+    first[span, CORE:] = pull.astype(BF16)
+    lifted = jnp.tile(narrow, (1, CORE // 128)) * mm(strip, window[:, :CORE])
+    basis[span, :] = lifted
+    first[span, :CORE] = lifted.astype(BF16)
+    block = lifted * root_row[0:1, :CORE]
+    gram[span, :CORE] = block.astype(BF16)
+    gram[:CORE, span] = block.astype(BF16).T
+    squares = 2.0 * squared(block)
+    root = root_column[span, 0:1]
+    if earlier is not None:
+        block = root * mm_nt(strip, earlier[...]) * root_row[0:1, CORE : CORE + RIM]
+        gram[span, CORE : CORE + RIM] = block.astype(BF16)
+        gram[CORE : CORE + RIM, span] = block.astype(BF16).T
+        squares += 2.0 * squared(block)
+    block = root * mm_nt(strip, strip) * root_row[0:1, span]
+    gram[span, span] = block.astype(BF16)
+    return strip, squares + squared(block), corners(block)
+
+
+def before_kernel(
+    before, own_sums, root_column, ratio_column, root_row, _window, _gram, _basis, _first, _pulls,
+    window, gram, basis, first, pulls, strip, sums,
+):
+    added, squares, trace = add_rim(
+        before, CORE, None, root_column, ratio_column, root_row, window, gram, basis, first, pulls
+    )
+    strip[...] = added
+    window[:, CORE : CORE + RIM] = added.T
+    sums[0:8, :] = own_sums[0:8, :] + squares
+    sums[8:16, :] = own_sums[8:16, :] + trace
 
 
 def analyse_kernel(
-    before, after, spread, state_mean, own_gram, own_basis, own_pulls, sums,
-    root_column, ratio_column, root_row,
-    out, fringe_t, fringe, gram, basis, pulls, first, second, third, fourth,
-):
-    live = (lax.broadcasted_iota(I32, (RIM, ROWS), 1) & (PADDED - 1)) < HELD
-    for rims, top in ((before, 0), (after, RIM)):
-        rows = slice(top, top + RIM)
-        tile = rims[...].astype(F32)
-        mean = jnp.sum(tile, axis=1, keepdims=True) / MEMBERS
-        fringe_t[rows, :] = jnp.where(live, tile - mean, 0.0).astype(BF16)
-        span = slice(CORE + top, CORE + top + RIM)
-        pulls[span, :] = ratio_column[span, :] - root_column[span, :] * mean
-    pulls[:CORE, :] = own_pulls[...]
-    gram[:CORE, :CORE] = own_gram[...]
-    basis[:CORE, :] = own_basis[...]
-    first[:CORE, :CORE] = own_basis[...].astype(BF16)
-    first[:, CORE:] = pulls[...].astype(BF16)
-
-    corner = lax.broadcasted_iota(I32, (128, 128), 0) == lax.broadcasted_iota(I32, (128, 128), 1)
-    squares = sums[0:1, 0:1]
-    trace = sums[8:9, 0:1]
-    for t in range(0, CORE, 128):
-        rows = slice(CORE + t, CORE + t + 128)
-        root = jnp.tile(root_column[rows, :], (1, CORE // 128))
-        strip = fringe_t[t : t + 128, :]
-        lifted = root * mm(strip, spread[...])
-        basis[rows, :] = lifted
-        first[rows, :CORE] = lifted.astype(BF16)
-        block = lifted * root_row[0:1, :CORE]
-        gram[rows, :CORE] = block.astype(BF16)
-        gram[:CORE, rows] = block.astype(BF16).T
-        squares += 2.0 * jnp.sum(block * block, keepdims=True)
-        block = root * mm_nt(strip, fringe_t[...]) * root_row[0:1, CORE:]
-        gram[rows, CORE:] = block.astype(BF16)
-        squares += jnp.sum(block * block, keepdims=True)
-        trace += jnp.sum(jnp.where(corner, block[:, t : t + 128], 0.0), keepdims=True)
+    after, strip, state_mean, sums, root_column, ratio_column, root_row,
+    _window, _gram, _basis, _first, _pulls,
+    window, gram, basis, first, pulls, out, second, third, fourth,
+):
+    added, squares, trace = add_rim(
+        after, CORE + RIM, strip, root_column, ratio_column, root_row, window, gram, basis, first,
+        pulls,
+    )
+    squares += sums[0:1, 0:1]
+    trace += sums[8:9, 0:1]
     draw = F32(MEMBERS - 1)
     inverse = 1.0 / (draw + 2.0 * squares / (draw + trace))
 
     a = draw * inverse
     r = 1.5 - 0.5 * a
     s = 1.5 - 0.5 * a * r * r
-
-    def step(source):
-        product = mm(gram[...], source[...])
-        return product[:, :CORE], product[:, CORE:]
-
-    def turn(t):
-        fringe[:, t : t + 128] = fringe_t[t : t + 128, :].T
-
-    turn(0)
-    pv, px = step(first)
-    v = (0.25 * inverse * inverse) * pv - (r * inverse) * basis[...]
-    second[:, :CORE] = v.astype(BF16)
-    second[:, CORE:] = (r * pulls[...] - (0.5 * inverse) * px).astype(BF16)
-
-    turn(128)
-    pv, px = step(second)
-    v = (0.5 * a) * second[:, :CORE].astype(F32) + (0.5 * inverse) * pv
-    v += (0.5 * r * r * inverse) * basis[...]
-    third[:, :CORE] = (-v).astype(BF16)
-    x = r * second[:, CORE:].astype(F32) - (0.5 * inverse) * px
-    third[:, CORE:] = x.astype(BF16)
-
-    turn(256)
-    pv, px = step(third)
-    v = r * third[:, :CORE].astype(F32) - (0.5 * inverse) * pv
-    v -= (0.5 * s * inverse) * basis[...]
-    fourth[:, :CORE] = v.astype(BF16)
-    x = (0.5 * a) * third[:, CORE:].astype(F32) + (0.5 * inverse) * px
-    fourth[:, CORE:] = (1.5 * pulls[...] - x).astype(BF16)
-    first[:, :CORE] = (jnp.tile(root_column[...], (1, CORE // 128)) * v).astype(BF16)
-
-    pv, px = step(fourth)
-    x = inverse * (r * fourth[:, CORE:].astype(F32) - (0.5 * inverse) * px)
+    halves = ((slice(0, 256), slice(0, 256)), (slice(256, CORE), slice(0, 128)))
+    last = slice(CORE, CORE + 128)
+
+    def product(source, h):
+        return mm(gram[...], source[:, h * 256 : (h + 1) * 256])
+
+    def one(h, p):
+        wide, part = halves[h]
+        v = (0.25 * inverse * inverse) * p[:, part] - (r * inverse) * basis[:, wide]
+        second[:, wide] = v.astype(BF16)
+        if h:
+            second[:, last] = (r * pulls[...] - (0.5 * inverse) * p[:, 128:]).astype(BF16)
+
+    def two(h, p):
+        wide, part = halves[h]
+        v = (-0.5 * a) * second[:, wide].astype(F32) - (0.5 * inverse) * p[:, part]
+        v -= (0.5 * r * r * inverse) * basis[:, wide]
+        third[:, wide] = v.astype(BF16)
+        if h:
+            x = r * second[:, last].astype(F32) - (0.5 * inverse) * p[:, 128:]
+            third[:, last] = x.astype(BF16)
+
+    def three(h, p):
+        wide, part = halves[h]
+        v = r * third[:, wide].astype(F32) - (0.5 * inverse) * p[:, part]
+        v -= (0.5 * s * inverse) * basis[:, wide]
+        fourth[:, wide] = v.astype(BF16)
+        first[:, wide] = (jnp.tile(root_column[...], (1, v.shape[1] // 128)) * v).astype(BF16)
+        if h:
+            x = (-0.5 * a) * third[:, last].astype(F32) - (0.5 * inverse) * p[:, 128:]
+            fourth[:, last] = (1.5 * pulls[...] + x).astype(BF16)
+
+    chain = (first, second, third, fourth)
+    waiting = [product(first, 0), product(first, 1)]
+    window[:, CORE + RIM :] = added.T
+    for k, finish in enumerate((one, two, three)):
+        for h in range(2):
+            finish(h, waiting[h])
+            waiting[h] = product(chain[k + 1], h)
+    x = r * fourth[:, last].astype(F32) - (0.5 * inverse) * waiting[1][:, 128:]
+    x *= inverse
     shift = []
-    for t in range(0, CORE, 128):
-        both = (r * s) * basis[:, t : t + 128] + pv[:, t : t + 128]
-        shift.append(jnp.sum(x * both, axis=0, keepdims=True))
+    for h, (wide, part) in enumerate(halves):
+        for t in range(part.start, part.stop, 128):
+            both = (r * s) * basis[:, h * 256 + t : h * 256 + t + 128] + waiting[h][:, t : t + 128]
+            shift.append(jnp.sum(x * both, axis=0, keepdims=True))
     base = state_mean[0:1, :] + jnp.concatenate(shift, axis=1)
     gain = jnp.sqrt(a)
     for t in range(0, ROWS, TILE):
-        own = spread[t : t + TILE, :]
-        moved = mm(own, first[:CORE, :CORE]) + mm(fringe[t : t + TILE, :], first[CORE:, :CORE])
-        moved += r * s * own.astype(F32)
-        out[t : t + TILE, :] = (base + gain * moved).astype(BF16)
-
-
-def call(kernel, name, in_specs, out_shape, out_specs=None, scratch_shapes=(), flops=0):
+        rows = slice(t, t + TILE)
+        moved = mm(window[rows, :], first[:, :CORE])
+        moved += r * s * window[rows, :CORE].astype(F32)
+        out[rows, :] = (base + gain * moved).astype(BF16)
+
+
+def call(
+    kernel, name, in_specs, out_shape, out_specs=None, scratch_shapes=(), flops=0, aliases=None
+):
     return pl.pallas_call(
         kernel,
         in_specs=in_specs,
         out_specs=out_specs or jax.tree.map(lambda _: vmem(), out_shape),
         out_shape=out_shape,
         scratch_shapes=list(scratch_shapes),
+        input_output_aliases=aliases or {},
         compiler_params=params(),
         cost_estimate=pl.CostEstimate(flops=flops, bytes_accessed=1 << 20, transcendentals=0),
         name=name,
@@ -332,29 +364,38 @@
     )(states, pick)
 
 
-def own_part(states, root_column, ratio_column, root_row):
-    return call(
+def growing():
+    return [
+        shape(ROWS, SPAN), shape(SPAN, SPAN), shape(SPAN, CORE, dtype=F32),
+        shape(SPAN, CORE + 128), shape(SPAN, 128, dtype=F32),
+    ]
+
+
+def own_part(states, prepared):
+    *grown, state_mean, sums = call(
         own_kernel, "own_part", [vmem()] * 4,
-        [shape(ROWS, CORE), shape(8, CORE, dtype=F32), shape(CORE, CORE),
-         shape(CORE, CORE, dtype=F32), shape(CORE, 128, dtype=F32), shape(16, 128, dtype=F32)],
+        growing() + [shape(8, CORE, dtype=F32), shape(16, 128, dtype=F32)],
         flops=2 * ROWS * CORE * CORE,
-    )(states, root_column, ratio_column, root_row)
-
-
-def analyse(before, after, own, prepared):
+    )(states, *prepared)
+    return grown, state_mean, sums
+
+
+def before_part(before, grown, sums, prepared):
+    *grown, strip, sums = call(
+        before_kernel, "before_part", [vmem()] * 10,
+        growing() + [shape(RIM, ROWS), shape(16, 128, dtype=F32)],
+        flops=2 * ROWS * RIM * (CORE + RIM), aliases={5 + k: k for k in range(5)},
+    )(before, sums, *prepared, *grown)
+    return grown, strip, sums
+
+
+def analyse(after, grown, strip, state_mean, sums, prepared):
     chain = pltpu.VMEM((SPAN, CORE + 128), BF16)
     return call(
-        analyse_kernel, "analyse", [vmem()] * 11, shape(ROWS, CORE),
-        scratch_shapes=[
-            pltpu.VMEM((CORE, ROWS), BF16),
-            pltpu.VMEM((ROWS, CORE), BF16),
-            pltpu.VMEM((SPAN, SPAN), BF16),
-            pltpu.VMEM((SPAN, CORE), F32),
-            pltpu.VMEM((SPAN, 128), F32),
-            chain, chain, chain, chain,
-        ],
-        flops=8 * SPAN * SPAN * CORE,
-    )(before, after, *own, *prepared)
+        analyse_kernel, "analyse", [vmem()] * 12, growing() + [shape(ROWS, CORE)],
+        scratch_shapes=[chain, chain, chain],
+        flops=8 * SPAN * SPAN * CORE, aliases={7 + k: k for k in range(5)},
+    )(after, strip, state_mean, sums, *prepared, *grown)[-1]
 
 
 def local(
@@ -381,8 +422,10 @@
     down = [(j, i) for i, j in up]
     before = lax.ppermute(rightward, axes, up)
     after = lax.ppermute(leftward, axes, down)
-    own = own_part(states, *prepared)
-    analysed = analyse(before, after, own, prepared).reshape(GROUP, PADDED, CORE)
+    grown, state_mean, sums = own_part(states, prepared)
+    grown, strip, sums = before_part(before, grown, sums, prepared)
+    analysed = analyse(after, grown, strip, state_mean, sums, prepared)
+    analysed = analysed.reshape(GROUP, PADDED, CORE)
     returned = lax.all_to_all(analysed, "member", split_axis=0, concat_axis=0, tiled=True)
     return jnp.transpose(leave(returned), (1, 0, 2))
 

time: 89.7 us -> 88.7 us (0.989)
    pallas_call x2 -> x3, Pallas kernels: 6.21 us -> 6.2 us  [the longest x1 4.44 us: analyse(): call(analyse_kernel, 'analyse', [vmem()] * 12, growing() + [shape(ROWS, C...]
where the time goes in v2:
time: 88.7 us; the launch traced here: 88.4 us
  blocking collectives  33.3 us (38%)
  starting transfers between devices  22.2 us (25%)
  waiting for transfers between devices  21 us (24%)
  Pallas kernels  10.7 us (12%)
  local copies, waits for them, and re-layouts  1.15 us (1%)
    all_to_all x1, blocking collectives, local(): lax.all_to_all(analysed, 'member', split_axis=0, concat_axis=0, tiled=True)  33.3 us
    all_to_all x1, waiting for transfers between devices, local(): lax.all_to_all(sent, 'member', split_axis=0, concat_axis=0, tiled=True)  17.9 us
    all_to_all x1, starting transfers between devices, local(): lax.all_to_all(sent, 'member', split_axis=0, concat_axis=0, tiled=True)  12.9 us
    ppermute x1, starting transfers between devices, local(): before = lax.ppermute(rightward, axes, up)  5.36 us
    pallas_call x1, Pallas kernels, analyse(): call(analyse_kernel, 'analyse', [vmem()] * 12, growing() + [shape(ROWS, C...  4.44 us
    ppermute x1, starting transfers between devices, local(): after = lax.ppermute(leftward, axes, down)  3.94 us
    ppermute x1, waiting for transfers between devices, local(): before = lax.ppermute(rightward, axes, up)  2.84 us
  transfers between devices with their start and end apart: 3, of which 3 were waited for; matrix products, arithmetic and copies ran while one was open for 0% of the time, Pallas kernels for 3%

profile of v2, /device:TPU:25, one launch (start us, length us, event | category | flops | bytes accessed | tf_op | source)
XLA Modules:
  0.0 88.4 jit_solution(13384842259558376215)
XLA Ops:
  0.0 0.0 copy-start
  0.0 1.1 %copy-done = bf16[32,30,384]{2,0,1:T(8,128)(2,1)S(1)} copy-done((bf16[32,30,384]{2,0,1:T(8,128)(2,1)S(1)}, bf16[32,30,384]{2,0,1:T(8,128)(2,1)}, u32[]{:S(2)}) %copy-start) | copy-done | bytes 737304
  1.1 0.0 copy-start.1
  1.1 0.0 copy-start.2
  1.1 0.0 copy-start.3
  1.1 0.0 copy-start.4
  1.1 0.0 copy-start.5
  1.1 0.0 copy-start.6
  1.1 0.0 copy-start.7
  1.2 1.3 %entry.1 = bf16[32,32,384]{2,1,0:T(8,128)(2,1)} custom-call(bf16[30,32,384]{2,1,0:T(8,128)(2,1)S(1)} %bitcast.7), custom_call_target="tpu_custom_call" | custom-call | flops 201326592 | bytes 1048576 | tf_op jit(solution)/shard_map/entry/pallas_call | solution.py:338
  2.5 12.9 %all-to-all-start = ((bf16[32,32,384]{2,1,0:T(8,128)(2,1)}), bf16[32,32,384]{2,1,0:T(8,128)(2,1)S(1)}, u32[]{:S(2)}, u32[]{:S(2)}) async-start(bf16[32,32,384]{2,1,0:T(8,128)(2,1)} %entry.1), calls=%async_computation | async-start | bytes 1572864 | tf_op jit(solution)/shard_map/all_to_all | solution.py:413
  15.4 0.0 copy-done.1
  15.4 0.0 copy-done.2
  15.4 0.0 copy-done.3
  15.4 0.0 copy-done.4
  15.4 0.0 copy-done.5
  15.4 0.0 copy-done.6
  15.4 0.0 copy-done.7
  15.5 1.3 %prepare.1 = (f32[768,128]{1,0:T(8,128)S(1)}, f32[768,128]{1,0:T(8,128)S(1)}, f32[8,768]{1,0:T(8,128)S(1)}, bf16[384,384]{1,0:T(8,128)(2,1)S(1)}) custom-call(s32[64]{0:T(128)S(1)} %copy-done.7, s32[32]{0:T(128)S(1)} %copy-done.5, s32[16]{0:T(128)S(1)} %copy-done.6, s32[32,640]{1,0:T(8,128)S(1)} %copy-done.1, f32[32,640]{1,0:T(8,128)S(1)} %copy-done.2, ...), custom_call_target="tpu_custom_call" | custom-call | flops 1966080 | bytes 1048576 | tf_op jit(solution)/shard_map/prepare/pallas_call | solution.py:352
  16.8 17.9 %all-to-all-done = bf16[32,32,384]{2,1,0:T(8,128)(2,1)S(1)} async-done(((bf16[32,32,384]{2,1,0:T(8,128)(2,1)}), bf16[32,32,384]{2,1,0:T(8,128)(2,1)S(1)}, u32[]{:S(2)}, u32[]{:S(2)}) %all-to-all-start) | async-done | bytes 786464 | tf_op jit(solution)/shard_map/all_to_all | solution.py:413
  34.6 0.6 extract.1
  35.2 5.4 %collective-permute-start.1 = (bf16[192,1024]{1,0:T(8,128)(2,1)S(1)}, bf16[192,1024]{1,0:T(8,128)(2,1)S(1)}, u32[]{:S(2)}, u32[]{:S(2)}) collective-permute-start(bf16[192,1024]{1,0:T(8,128)(2,1)S(1)} %get-tuple-element.28), channel_id=1, source_target_pairs={{0,128},{128,144},{144,272},{272,256},{256,368},{368,352},{352,224... | collective-permute-start | bytes 1179656 | tf_op jit(solution)/shard_map/ppermute | solution.py:423
  40.6 3.9 %collective-permute-start = (bf16[192,1024]{1,0:T(8,128)(2,1)S(1)}, bf16[192,1024]{1,0:T(8,128)(2,1)S(1)}, u32[]{:S(2)}, u32[]{:S(2)}) collective-permute-start(bf16[192,1024]{1,0:T(8,128)(2,1)S(1)} %get-tuple-element.27), channel_id=1, source_target_pairs={{128,0},{144,128},{272,144},{256,272},{368,256},{352,368},{224,352... | collective-permute-start | bytes 1179656 | tf_op jit(solution)/shard_map/ppermute | solution.py:424
  44.6 1.0 %own_part.1 = (bf16[1024,768]{1,0:T(8,128)(2,1)S(1)}, bf16[768,768]{1,0:T(8,128)(2,1)S(1)}, f32[768,384]{1,0:T(8,128)S(1)}, bf16[768,512]{1,0:T(8,128)(2,1)S(1)}...) custom-call(bf16[1024,384]{1,0:T(8,128)(2,1)S(1)} %bitcast.5, ...), custom_call_target="tpu_custom_call" | custom-call | flops 301989888 | bytes 1048576 | tf_op jit(solution)/shard_map/own_part/pallas_call | solution.py:375
  45.5 2.8 %collective-permute-done.1.before = bf16[192,1024]{1,0:T(8,128)(2,1)S(1)} collective-permute-done((bf16[192,1024]{1,0:T(8,128)(2,1)S(1)}, bf16[192,1024]{1,0:T(8,128)(2,1)S(1)}, u32[]{:S(2)}, u32[]{:S(2)}) %collective-permute-start.1) | collective-permute-done | bytes 393248 | tf_op jit(solution)/shard_map/ppermute | solution.py:423
  48.4 0.8 before_part.1
  49.2 0.3 collective-permute-done.after
  49.4 4.4 %analyse.1 = (bf16[1024,768]{1,0:T(8,128)(2,1)S(1)}, bf16[768,768]{1,0:T(8,128)(2,1)S(1)}, f32[768,384]{1,0:T(8,128)S(1)}, bf16[768,512]{1,0:T(8,128)(2,1)S(1)},...) custom-call(bf16[192,1024]{1,0:T(8,128)(2,1)S(1)} %collective-permut, ...), custom_call_target="tpu_custom_call", output_to_operand_aliasing={{0}: (7, {}), {1}: (8, {}), {2}: (9, {}), {3}: (10, {}), {4... | custom-call | flops 1811939328 | bytes 1048576 | tf_op jit(solution)/shard_map/analyse/pallas_call | solution.py:394
  53.9 33.3 %all_to_all.10.analysed = bf16[32,32,384]{2,1,0:T(8,128)(2,1)S(1)} all-to-all(bf16[32,32,384]{2,1,0:T(8,128)(2,1)S(1)} %bitcast.6), channel_id=1, replica_groups=mesh['member'=32,'patch'=16] {'member'}, dimensions={0} | all-to-all | bytes 1572864 | tf_op jit(solution)/shard_map/all_to_all | solution.py:429
  87.2 1.2 %exit.1 = bf16[30,32,384]{2,1,0:T(8,128)(2,1)} custom-call(bf16[32,32,384]{2,1,0:T(8,128)(2,1)S(1)} %all_to_all.10.analysed), custom_call_target="tpu_custom_call" | custom-call | flops 201326592 | bytes 1048576 | tf_op jit(solution)/shard_map/exit/pallas_call | solution.py:344
Async XLA Ops:
  0.0 1.1 %copy-start = (bf16[32,30,384]{2,0,1:T(8,128)(2,1)S(1)}, bf16[32,30,384]{2,0,1:T(8,128)(2,1)}, u32[]{:S(2)}) copy-start(bf16[32,30,384]{2,0,1:T(8,128)(2,1)} %param.8) | copy-start | bytes 2211844
  1.1 14.3 %copy-start.1 = (s32[32,640]{1,0:T(8,128)S(1)}, s32[32,640]{1,0:T(8,128)}, u32[]{:S(2)}) copy-start(s32[32,640]{1,0:T(8,128)} %location.1) | copy-start | bytes 245764
  1.1 14.3 %copy-start.2 = (f32[32,640]{1,0:T(8,128)S(1)}, f32[32,640]{1,0:T(8,128)}, u32[]{:S(2)}) copy-start(f32[32,640]{1,0:T(8,128)} %datum.1) | copy-start | bytes 245764
  1.1 14.3 %copy-start.3 = (f32[32,640]{1,0:T(8,128)S(1)}, f32[32,640]{1,0:T(8,128)}, u32[]{:S(2)}) copy-start(f32[32,640]{1,0:T(8,128)} %error_spread.1) | copy-start | bytes 245764
  1.1 14.3 %copy-start.4 = (s32[32,640]{1,0:T(8,128)S(1)}, s32[32,640]{1,0:T(8,128)}, u32[]{:S(2)}) copy-start(s32[32,640]{1,0:T(8,128)} %band.1) | copy-start | bytes 245764
  1.1 14.3 %copy-start.5 = (s32[32]{0:T(128)S(1)}, s32[32]{0:T(128)}, u32[]{:S(2)}) copy-start(s32[32]{0:T(128)} %tally.1) | copy-start | bytes 388
  1.1 14.3 %copy-start.6 = (s32[16]{0:T(128)S(1)}, s32[16]{0:T(128)}, u32[]{:S(2)}) copy-start(s32[16]{0:T(128)} %taper.1) | copy-start | bytes 196
  1.1 14.3 %copy-start.7 = (s32[64]{0:T(128)S(1)}, s32[64]{0:T(128)}, u32[]{:S(2)}) copy-start(s32[64]{0:T(128)} %constant.2.clone.hosted) | copy-start | bytes 772
  2.5 32.1 %all-to-all-start = ((bf16[32,32,384]{2,1,0:T(8,128)(2,1)}), bf16[32,32,384]{2,1,0:T(8,128)(2,1)S(1)}, u32[]{:S(2)}, u32[]{:S(2)}) async-start(bf16[32,32,384]{2,1,0:T(8,128)(2,1)} %entry.1), calls=%async_computation | async-start | bytes 1572864 | tf_op jit(solution)/shard_map/all_to_all | solution.py:413
  35.2 13.1 %collective-permute-start.1 = (bf16[192,1024]{1,0:T(8,128)(2,1)S(1)}, bf16[192,1024]{1,0:T(8,128)(2,1)S(1)}, u32[]{:S(2)}, u32[]{:S(2)}) collective-permute-start(bf16[192,1024]{1,0:T(8,128)(2,1)S(1)} %get-tuple-element.28), channel_id=1, source_target_pairs={{0,128},{128,144},{144,272},{272,256},{256,368},{368,352},{352,224... | collective-permute-start | bytes 1179656 | tf_op jit(solution)/shard_map/ppermute | solution.py:423
  40.6 8.8 %collective-permute-start = (bf16[192,1024]{1,0:T(8,128)(2,1)S(1)}, bf16[192,1024]{1,0:T(8,128)(2,1)S(1)}, u32[]{:S(2)}, u32[]{:S(2)}) collective-permute-start(bf16[192,1024]{1,0:T(8,128)(2,1)S(1)} %get-tuple-element.27), channel_id=1, source_target_pairs={{128,0},{144,128},{272,144},{256,272},{368,256},{352,368},{224,352... | collective-permute-start | bytes 1179656 | tf_op jit(solution)/shard_map/ppermute | solution.py:424

commit v3 on v2

--- a/solution.py
+++ b/solution.py
@@ -177,26 +177,42 @@
     return jnp.sum(block * block, keepdims=True)
 
 
+def scales(peak):
+    exponent = jnp.floor(jnp.log2(jnp.where(peak > 0.0, peak, 1.0)))
+    exponent = jnp.minimum(jnp.maximum(exponent, -100.0), 120.0)
+    return jnp.exp2(exponent), jnp.exp2(-exponent)
+
+
 def own_kernel(
     states, root_column, ratio_column, root_row,
-    window, gram, basis, first, pulls, state_mean, sums,
+    window, gram, basis, first, pulls, weight_column, weight_row, state_mean, sums,
 ):
     total = jnp.zeros((1, CORE), F32)
     for t in range(0, ROWS, TILE):
         total += jnp.sum(states[t : t + TILE, :].astype(F32), axis=0, keepdims=True)
     mean = total / MEMBERS
-    state_mean[...] = jnp.broadcast_to(mean, (8, CORE))
     live = (lax.broadcasted_iota(I32, (TILE, CORE), 0) & (PADDED - 1)) < HELD
+    peak = jnp.zeros((1, CORE), F32)
+    for t in range(0, ROWS, TILE):
+        tile = jnp.where(live, states[t : t + TILE, :].astype(F32) - mean, 0.0)
+        peak = jnp.maximum(peak, jnp.max(jnp.abs(tile), axis=0, keepdims=True))
+    scale, inverse = scales(peak)
+    state_mean[0:1, :] = mean
+    state_mean[1:2, :] = scale
     covariance = jnp.zeros((CORE, CORE), F32)
     for t in range(0, ROWS, TILE):
-        tile = jnp.where(live, states[t : t + TILE, :].astype(F32) - mean, 0.0)
+        tile = jnp.where(live, (states[t : t + TILE, :].astype(F32) - mean) * inverse, 0.0)
         window[t : t + TILE, :CORE] = tile.astype(BF16)
         covariance += mm(tile.T.astype(BF16), tile.astype(BF16))
     root = root_column[:CORE, :]
-    lifted = jnp.tile(root, (1, CORE // 128)) * covariance
+    weight = root * jnp.broadcast_to(scale, (128, CORE)).T
+    weight_column[:CORE, :] = weight
+    across = root_row[0:1, :CORE] * scale
+    weight_row[0:1, :CORE] = across
+    lifted = jnp.tile(weight, (1, CORE // 128)) * covariance
     basis[:CORE, :] = lifted
     first[:CORE, :CORE] = lifted.astype(BF16)
-    block = lifted * root_row[0:1, :CORE]
+    block = lifted * across
     gram[:CORE, :CORE] = block.astype(BF16)
     pull = ratio_column[:CORE, :] - root * jnp.broadcast_to(mean, (128, CORE)).T
     pulls[:CORE, :] = pull
@@ -205,40 +221,51 @@
     sums[8:16, :] = jnp.broadcast_to(corners(block), (8, 128))
 
 
-def add_rim(rims, top, earlier, root_column, ratio_column, root_row, window, gram, basis, first, pulls):
+def add_rim(
+    rims, top, earlier, root_column, ratio_column,
+    window, gram, basis, first, pulls, weight_column, weight_row,
+):
     span = slice(top, top + RIM)
     live = (lax.broadcasted_iota(I32, (RIM, ROWS), 1) & (PADDED - 1)) < HELD
     tile = rims[...].astype(F32)
     mean = jnp.sum(tile, axis=1, keepdims=True) / MEMBERS
-    strip = jnp.where(live, tile - mean, 0.0).astype(BF16)
-    narrow = root_column[span, :]
-    pull = ratio_column[span, :] - narrow * mean
+    tile = jnp.where(live, tile - mean, 0.0)
+    scale, inverse = scales(jnp.max(jnp.abs(tile), axis=1, keepdims=True))
+    strip = (tile * inverse).astype(BF16)
+    root = root_column[span, :]
+    pull = ratio_column[span, :] - root * mean
     pulls[span, :] = pull
     first[span, CORE:] = pull.astype(BF16)
-    lifted = jnp.tile(narrow, (1, CORE // 128)) * mm(strip, window[:, :CORE])
+    weight = root * scale
+    weight_column[span, :] = weight
+    across = weight.T[0:1, :]
+    weight_row[0:1, span] = across
+    lifted = jnp.tile(weight, (1, CORE // 128)) * mm(strip, window[:, :CORE])
     basis[span, :] = lifted
     first[span, :CORE] = lifted.astype(BF16)
-    block = lifted * root_row[0:1, :CORE]
+    block = lifted * weight_row[0:1, :CORE]
     gram[span, :CORE] = block.astype(BF16)
     gram[:CORE, span] = block.astype(BF16).T
     squares = 2.0 * squared(block)
-    root = root_column[span, 0:1]
+    weight = weight[:, 0:1]
     if earlier is not None:
-        block = root * mm_nt(strip, earlier[...]) * root_row[0:1, CORE : CORE + RIM]
+        block = weight * mm_nt(strip, earlier[...]) * weight_row[0:1, CORE : CORE + RIM]
         gram[span, CORE : CORE + RIM] = block.astype(BF16)
         gram[CORE : CORE + RIM, span] = block.astype(BF16).T
         squares += 2.0 * squared(block)
-    block = root * mm_nt(strip, strip) * root_row[0:1, span]
+    block = weight * mm_nt(strip, strip) * across
     gram[span, span] = block.astype(BF16)
     return strip, squares + squared(block), corners(block)
 
 
 def before_kernel(
-    before, own_sums, root_column, ratio_column, root_row, _window, _gram, _basis, _first, _pulls,
-    window, gram, basis, first, pulls, strip, sums,
+    before, own_sums, root_column, ratio_column,
+    _window, _gram, _basis, _first, _pulls, _weight_column, _weight_row,
+    window, gram, basis, first, pulls, weight_column, weight_row, strip, sums,
 ):
     added, squares, trace = add_rim(
-        before, CORE, None, root_column, ratio_column, root_row, window, gram, basis, first, pulls
+        before, CORE, None, root_column, ratio_column,
+        window, gram, basis, first, pulls, weight_column, weight_row,
     )
     strip[...] = added
     window[:, CORE : CORE + RIM] = added.T
@@ -247,13 +274,13 @@
 
 
 def analyse_kernel(
-    after, strip, state_mean, sums, root_column, ratio_column, root_row,
-    _window, _gram, _basis, _first, _pulls,
-    window, gram, basis, first, pulls, out, second, third, fourth,
+    after, strip, state_mean, sums, root_column, ratio_column,
+    _window, _gram, _basis, _first, _pulls, _weight_column, _weight_row,
+    window, gram, basis, first, pulls, weight_column, weight_row, out, second, third, fourth,
 ):
     added, squares, trace = add_rim(
-        after, CORE + RIM, strip, root_column, ratio_column, root_row, window, gram, basis, first,
-        pulls,
+        after, CORE + RIM, strip, root_column, ratio_column,
+        window, gram, basis, first, pulls, weight_column, weight_row,
     )
     squares += sums[0:1, 0:1]
     trace += sums[8:9, 0:1]
@@ -290,7 +317,7 @@
         v = r * third[:, wide].astype(F32) - (0.5 * inverse) * p[:, part]
         v -= (0.5 * s * inverse) * basis[:, wide]
         fourth[:, wide] = v.astype(BF16)
-        first[:, wide] = (jnp.tile(root_column[...], (1, v.shape[1] // 128)) * v).astype(BF16)
+        first[:, wide] = (jnp.tile(weight_column[...], (1, v.shape[1] // 128)) * v).astype(BF16)
         if h:
             x = (-0.5 * a) * third[:, last].astype(F32) - (0.5 * inverse) * p[:, 128:]
             fourth[:, last] = (1.5 * pulls[...] + x).astype(BF16)
@@ -309,8 +336,9 @@
         for t in range(part.start, part.stop, 128):
             both = (r * s) * basis[:, h * 256 + t : h * 256 + t + 128] + waiting[h][:, t : t + 128]
             shift.append(jnp.sum(x * both, axis=0, keepdims=True))
-    base = state_mean[0:1, :] + jnp.concatenate(shift, axis=1)
-    gain = jnp.sqrt(a)
+    scale = state_mean[1:2, :]
+    base = state_mean[0:1, :] + scale * jnp.concatenate(shift, axis=1)
+    gain = jnp.sqrt(a) * scale
     for t in range(0, ROWS, TILE):
         rows = slice(t, t + TILE)
         moved = mm(window[rows, :], first[:, :CORE])
@@ -368,6 +396,7 @@
     return [
         shape(ROWS, SPAN), shape(SPAN, SPAN), shape(SPAN, CORE, dtype=F32),
         shape(SPAN, CORE + 128), shape(SPAN, 128, dtype=F32),
+        shape(SPAN, 128, dtype=F32), shape(8, SPAN, dtype=F32),
     ]
 
 
@@ -382,20 +411,20 @@
 
 def before_part(before, grown, sums, prepared):
     *grown, strip, sums = call(
-        before_kernel, "before_part", [vmem()] * 10,
+        before_kernel, "before_part", [vmem()] * 11,
         growing() + [shape(RIM, ROWS), shape(16, 128, dtype=F32)],
-        flops=2 * ROWS * RIM * (CORE + RIM), aliases={5 + k: k for k in range(5)},
-    )(before, sums, *prepared, *grown)
+        flops=2 * ROWS * RIM * (CORE + RIM), aliases={4 + k: k for k in range(7)},
+    )(before, sums, *prepared[:2], *grown)
     return grown, strip, sums
 
 
 def analyse(after, grown, strip, state_mean, sums, prepared):
     chain = pltpu.VMEM((SPAN, CORE + 128), BF16)
     return call(
-        analyse_kernel, "analyse", [vmem()] * 12, growing() + [shape(ROWS, CORE)],
+        analyse_kernel, "analyse", [vmem()] * 13, growing() + [shape(ROWS, CORE)],
         scratch_shapes=[chain, chain, chain],
-        flops=8 * SPAN * SPAN * CORE, aliases={7 + k: k for k in range(5)},
-    )(after, strip, state_mean, sums, *prepared, *grown)[-1]
+        flops=8 * SPAN * SPAN * CORE, aliases={6 + k: k for k in range(7)},
+    )(after, strip, state_mean, sums, *prepared[:2], *grown)[-1]
 
 
 def local(

time: 88.7 us -> 88.9 us (level)
  transfers between devices with their start and end apart: 3 -> 3, of which waited for: 3 -> 3; matrix products, arithmetic and copies ran while one was open for 0% -> 0% of each run, Pallas kernels for 3% -> 4%
where the time goes in v3:
time: 88.9 us; the launch traced here: 88.5 us
  blocking collectives  33.3 us (37%)
  starting transfers between devices  22.2 us (25%)
  waiting for transfers between devices  20.6 us (23%)
  Pallas kernels  11.2 us (13%)
  local copies, waits for them, and re-layouts  1.15 us (1%)
    all_to_all x1, blocking collectives, local(): lax.all_to_all(analysed, 'member', split_axis=0, concat_axis=0, tiled=True)  33.3 us
    all_to_all x1, waiting for transfers between devices, local(): lax.all_to_all(sent, 'member', split_axis=0, concat_axis=0, tiled=True)  17.9 us
    all_to_all x1, starting transfers between devices, local(): lax.all_to_all(sent, 'member', split_axis=0, concat_axis=0, tiled=True)  12.9 us
    ppermute x1, starting transfers between devices, local(): before = lax.ppermute(rightward, axes, up)  5.36 us
    pallas_call x1, Pallas kernels, analyse(): call(analyse_kernel, 'analyse', [vmem()] * 13, growing() + [shape(ROWS, C...  4.62 us
    ppermute x1, starting transfers between devices, local(): after = lax.ppermute(leftward, axes, down)  3.94 us
    ppermute x1, waiting for transfers between devices, local(): before = lax.ppermute(rightward, axes, up)  2.62 us
  transfers between devices with their start and end apart: 3, of which 3 were waited for; matrix products, arithmetic and copies ran while one was open for 0% of the time, Pallas kernels for 4%

profile of v3, /device:TPU:25, one launch (start us, length us, event | category | flops | bytes accessed | tf_op | source)
XLA Modules:
  0.0 88.5 jit_solution(11584096838173413350)
XLA Ops:
  0.0 0.0 copy-start
  0.0 1.1 %copy-done = bf16[32,30,384]{2,0,1:T(8,128)(2,1)S(1)} copy-done((bf16[32,30,384]{2,0,1:T(8,128)(2,1)S(1)}, bf16[32,30,384]{2,0,1:T(8,128)(2,1)}, u32[]{:S(2)}) %copy-start) | copy-done | bytes 737304
  1.1 0.0 copy-start.1
  1.1 0.0 copy-start.2
  1.1 0.0 copy-start.3
  1.1 0.0 copy-start.4
  1.1 0.0 copy-start.5
  1.1 0.0 copy-start.6
  1.1 0.0 copy-start.7
  1.2 1.3 %entry.1 = bf16[32,32,384]{2,1,0:T(8,128)(2,1)} custom-call(bf16[30,32,384]{2,1,0:T(8,128)(2,1)S(1)} %bitcast.7), custom_call_target="tpu_custom_call" | custom-call | flops 201326592 | bytes 1048576 | tf_op jit(solution)/shard_map/entry/pallas_call | solution.py:366
  2.5 12.9 %all-to-all-start = ((bf16[32,32,384]{2,1,0:T(8,128)(2,1)}), bf16[32,32,384]{2,1,0:T(8,128)(2,1)S(1)}, u32[]{:S(2)}, u32[]{:S(2)}) async-start(bf16[32,32,384]{2,1,0:T(8,128)(2,1)} %entry.1), calls=%async_computation | async-start | bytes 1572864 | tf_op jit(solution)/shard_map/all_to_all | solution.py:442
  15.4 0.0 copy-done.1
  15.4 0.0 copy-done.2
  15.4 0.0 copy-done.3
  15.4 0.0 copy-done.4
  15.4 0.0 copy-done.5
  15.4 0.0 copy-done.6
  15.4 0.0 copy-done.7
  15.5 1.3 %prepare.1 = (f32[768,128]{1,0:T(8,128)S(1)}, f32[768,128]{1,0:T(8,128)S(1)}, f32[8,768]{1,0:T(8,128)S(1)}, bf16[384,384]{1,0:T(8,128)(2,1)S(1)}) custom-call(s32[64]{0:T(128)S(1)} %copy-done.7, s32[32]{0:T(128)S(1)} %copy-done.5, s32[16]{0:T(128)S(1)} %copy-done.6, s32[32,640]{1,0:T(8,128)S(1)} %copy-done.1, f32[32,640]{1,0:T(8,128)S(1)} %copy-done.2, ...), custom_call_target="tpu_custom_call" | custom-call | flops 1966080 | bytes 1048576 | tf_op jit(solution)/shard_map/prepare/pallas_call | solution.py:380
  16.8 17.9 %all-to-all-done = bf16[32,32,384]{2,1,0:T(8,128)(2,1)S(1)} async-done(((bf16[32,32,384]{2,1,0:T(8,128)(2,1)}), bf16[32,32,384]{2,1,0:T(8,128)(2,1)S(1)}, u32[]{:S(2)}, u32[]{:S(2)}) %all-to-all-start) | async-done | bytes 786464 | tf_op jit(solution)/shard_map/all_to_all | solution.py:442
  34.6 0.6 extract.1
  35.2 5.4 %collective-permute-start.1 = (bf16[192,1024]{1,0:T(8,128)(2,1)S(1)}, bf16[192,1024]{1,0:T(8,128)(2,1)S(1)}, u32[]{:S(2)}, u32[]{:S(2)}) collective-permute-start(bf16[192,1024]{1,0:T(8,128)(2,1)S(1)} %get-tuple-element.32), channel_id=1, source_target_pairs={{0,128},{128,144},{144,272},{272,256},{256,368},{368,352},{352,224... | collective-permute-start | bytes 1179656 | tf_op jit(solution)/shard_map/ppermute | solution.py:452
  40.6 3.9 %collective-permute-start = (bf16[192,1024]{1,0:T(8,128)(2,1)S(1)}, bf16[192,1024]{1,0:T(8,128)(2,1)S(1)}, u32[]{:S(2)}, u32[]{:S(2)}) collective-permute-start(bf16[192,1024]{1,0:T(8,128)(2,1)S(1)} %get-tuple-element.31), channel_id=1, source_target_pairs={{128,0},{144,128},{272,144},{256,272},{368,256},{352,368},{224,352... | collective-permute-start | bytes 1179656 | tf_op jit(solution)/shard_map/ppermute | solution.py:453
  44.6 1.2 %own_part.1 = (bf16[1024,768]{1,0:T(8,128)(2,1)S(1)}, bf16[768,768]{1,0:T(8,128)(2,1)S(1)}, f32[768,384]{1,0:T(8,128)S(1)}, bf16[768,512]{1,0:T(8,128)(2,1)S(1)}...) custom-call(bf16[1024,384]{1,0:T(8,128)(2,1)S(1)} %bitcast.5, ...), custom_call_target="tpu_custom_call" | custom-call | flops 301989888 | bytes 1048576 | tf_op jit(solution)/shard_map/own_part/pallas_call | solution.py:404
  45.8 2.6 %collective-permute-done.1.before = bf16[192,1024]{1,0:T(8,128)(2,1)S(1)} collective-permute-done((bf16[192,1024]{1,0:T(8,128)(2,1)S(1)}, bf16[192,1024]{1,0:T(8,128)(2,1)S(1)}, u32[]{:S(2)}, u32[]{:S(2)}) %collective-permute-start.1) | collective-permute-done | bytes 393248 | tf_op jit(solution)/shard_map/ppermute | solution.py:452
  48.4 0.9 %before_part.1 = (bf16[1024,768]{1,0:T(8,128)(2,1)S(1)}, bf16[768,768]{1,0:T(8,128)(2,1)S(1)}, f32[768,384]{1,0:T(8,128)S(1)}, bf16[768,512]{1,0:T(8,128)(2,1)S(...) custom-call(bf16[192,1024]{1,0:T(8,128)(2,1)S(1)} %collective-permut, ...), custom_call_target="tpu_custom_call", output_to_operand_aliasing={{0}: (4, {}), {1}: (5, {}), {2}: (6, {}), {3}: (7, {}), {4}... | custom-call | flops 226492416 | bytes 1048576 | tf_op jit(solution)/shard_map/before_part/pallas_call | solution.py:413
  49.3 0.1 collective-permute-done.after
  49.4 4.6 %analyse.1 = (bf16[1024,768]{1,0:T(8,128)(2,1)S(1)}, bf16[768,768]{1,0:T(8,128)(2,1)S(1)}, f32[768,384]{1,0:T(8,128)S(1)}, bf16[768,512]{1,0:T(8,128)(2,1)S(1)},...) custom-call(bf16[192,1024]{1,0:T(8,128)(2,1)S(1)} %collective-permut, ...), custom_call_target="tpu_custom_call", output_to_operand_aliasing={{0}: (6, {}), {1}: (7, {}), {2}: (8, {}), {3}: (9, {}), {4}... | custom-call | flops 1811939328 | bytes 1048576 | tf_op jit(solution)/shard_map/analyse/pallas_call | solution.py:423
  54.1 33.3 %all_to_all.10.analysed = bf16[32,32,384]{2,1,0:T(8,128)(2,1)S(1)} all-to-all(bf16[32,32,384]{2,1,0:T(8,128)(2,1)S(1)} %bitcast.6), channel_id=1, replica_groups=mesh['member'=32,'patch'=16] {'member'}, dimensions={0} | all-to-all | bytes 1572864 | tf_op jit(solution)/shard_map/all_to_all | solution.py:458
  87.3 1.2 %exit.1 = bf16[30,32,384]{2,1,0:T(8,128)(2,1)} custom-call(bf16[32,32,384]{2,1,0:T(8,128)(2,1)S(1)} %all_to_all.10.analysed), custom_call_target="tpu_custom_call" | custom-call | flops 201326592 | bytes 1048576 | tf_op jit(solution)/shard_map/exit/pallas_call | solution.py:372
Async XLA Ops:
  0.0 1.1 %copy-start = (bf16[32,30,384]{2,0,1:T(8,128)(2,1)S(1)}, bf16[32,30,384]{2,0,1:T(8,128)(2,1)}, u32[]{:S(2)}) copy-start(bf16[32,30,384]{2,0,1:T(8,128)(2,1)} %param.8) | copy-start | bytes 2211844
  1.1 14.3 %copy-start.1 = (s32[32,640]{1,0:T(8,128)S(1)}, s32[32,640]{1,0:T(8,128)}, u32[]{:S(2)}) copy-start(s32[32,640]{1,0:T(8,128)} %location.1) | copy-start | bytes 245764
  1.1 14.3 %copy-start.2 = (f32[32,640]{1,0:T(8,128)S(1)}, f32[32,640]{1,0:T(8,128)}, u32[]{:S(2)}) copy-start(f32[32,640]{1,0:T(8,128)} %datum.1) | copy-start | bytes 245764
  1.1 14.3 %copy-start.3 = (f32[32,640]{1,0:T(8,128)S(1)}, f32[32,640]{1,0:T(8,128)}, u32[]{:S(2)}) copy-start(f32[32,640]{1,0:T(8,128)} %error_spread.1) | copy-start | bytes 245764
  1.1 14.3 %copy-start.4 = (s32[32,640]{1,0:T(8,128)S(1)}, s32[32,640]{1,0:T(8,128)}, u32[]{:S(2)}) copy-start(s32[32,640]{1,0:T(8,128)} %band.1) | copy-start | bytes 245764
  1.1 14.3 %copy-start.5 = (s32[32]{0:T(128)S(1)}, s32[32]{0:T(128)}, u32[]{:S(2)}) copy-start(s32[32]{0:T(128)} %tally.1) | copy-start | bytes 388
  1.1 14.3 %copy-start.6 = (s32[16]{0:T(128)S(1)}, s32[16]{0:T(128)}, u32[]{:S(2)}) copy-start(s32[16]{0:T(128)} %taper.1) | copy-start | bytes 196
  1.1 14.3 %copy-start.7 = (s32[64]{0:T(128)S(1)}, s32[64]{0:T(128)}, u32[]{:S(2)}) copy-start(s32[64]{0:T(128)} %constant.2.clone.hosted) | copy-start | bytes 772
  2.5 32.1 %all-to-all-start = ((bf16[32,32,384]{2,1,0:T(8,128)(2,1)}), bf16[32,32,384]{2,1,0:T(8,128)(2,1)S(1)}, u32[]{:S(2)}, u32[]{:S(2)}) async-start(bf16[32,32,384]{2,1,0:T(8,128)(2,1)} %entry.1), calls=%async_computation | async-start | bytes 1572864 | tf_op jit(solution)/shard_map/all_to_all | solution.py:442
  35.2 13.1 %collective-permute-start.1 = (bf16[192,1024]{1,0:T(8,128)(2,1)S(1)}, bf16[192,1024]{1,0:T(8,128)(2,1)S(1)}, u32[]{:S(2)}, u32[]{:S(2)}) collective-permute-start(bf16[192,1024]{1,0:T(8,128)(2,1)S(1)} %get-tuple-element.32), channel_id=1, source_target_pairs={{0,128},{128,144},{144,272},{272,256},{256,368},{368,352},{352,224... | collective-permute-start | bytes 1179656 | tf_op jit(solution)/shard_map/ppermute | solution.py:452
  40.6 8.8 %collective-permute-start = (bf16[192,1024]{1,0:T(8,128)(2,1)S(1)}, bf16[192,1024]{1,0:T(8,128)(2,1)S(1)}, u32[]{:S(2)}, u32[]{:S(2)}) collective-permute-start(bf16[192,1024]{1,0:T(8,128)(2,1)S(1)} %get-tuple-element.31), channel_id=1, source_target_pairs={{128,0},{144,128},{272,144},{256,272},{368,256},{352,368},{224,352... | collective-permute-start | bytes 1179656 | tf_op jit(solution)/shard_map/ppermute | solution.py:453

commit v4 on v3

--- a/solution.py
+++ b/solution.py
@@ -207,8 +207,10 @@
     root = root_column[:CORE, :]
     weight = root * jnp.broadcast_to(scale, (128, CORE)).T
     weight_column[:CORE, :] = weight
+    weight_column[CORE:, :] = root_column[CORE:, :]
     across = root_row[0:1, :CORE] * scale
     weight_row[0:1, :CORE] = across
+    weight_row[0:1, CORE:] = root_row[0:1, CORE:]
     lifted = jnp.tile(weight, (1, CORE // 128)) * covariance
     basis[:CORE, :] = lifted
     first[:CORE, :CORE] = lifted.astype(BF16)
@@ -222,24 +224,19 @@
 
 
 def add_rim(
-    rims, top, earlier, root_column, ratio_column,
+    rims, top, earlier, ratio_column,
     window, gram, basis, first, pulls, weight_column, weight_row,
 ):
     span = slice(top, top + RIM)
     live = (lax.broadcasted_iota(I32, (RIM, ROWS), 1) & (PADDED - 1)) < HELD
     tile = rims[...].astype(F32)
     mean = jnp.sum(tile, axis=1, keepdims=True) / MEMBERS
-    tile = jnp.where(live, tile - mean, 0.0)
-    scale, inverse = scales(jnp.max(jnp.abs(tile), axis=1, keepdims=True))
-    strip = (tile * inverse).astype(BF16)
-    root = root_column[span, :]
-    pull = ratio_column[span, :] - root * mean
+    weight = weight_column[span, :]
+    seen = jnp.where(weight[:, 0:1] > 0.0, 1.0, 0.0)
+    strip = jnp.where(live, (tile - mean) * seen, 0.0).astype(BF16)
+    pull = ratio_column[span, :] - weight * mean
     pulls[span, :] = pull
     first[span, CORE:] = pull.astype(BF16)
-    weight = root * scale
-    weight_column[span, :] = weight
-    across = weight.T[0:1, :]
-    weight_row[0:1, span] = across
     lifted = jnp.tile(weight, (1, CORE // 128)) * mm(strip, window[:, :CORE])
     basis[span, :] = lifted
     first[span, :CORE] = lifted.astype(BF16)
@@ -253,18 +250,18 @@
         gram[span, CORE : CORE + RIM] = block.astype(BF16)
         gram[CORE : CORE + RIM, span] = block.astype(BF16).T
         squares += 2.0 * squared(block)
-    block = weight * mm_nt(strip, strip) * across
+    block = weight * mm_nt(strip, strip) * weight_row[0:1, span]
     gram[span, span] = block.astype(BF16)
     return strip, squares + squared(block), corners(block)
 
 
 def before_kernel(
-    before, own_sums, root_column, ratio_column,
+    before, own_sums, ratio_column,
     _window, _gram, _basis, _first, _pulls, _weight_column, _weight_row,
     window, gram, basis, first, pulls, weight_column, weight_row, strip, sums,
 ):
     added, squares, trace = add_rim(
-        before, CORE, None, root_column, ratio_column,
+        before, CORE, None, ratio_column,
         window, gram, basis, first, pulls, weight_column, weight_row,
     )
     strip[...] = added
@@ -274,12 +271,12 @@
 
 
 def analyse_kernel(
-    after, strip, state_mean, sums, root_column, ratio_column,
+    after, strip, state_mean, sums, ratio_column,
     _window, _gram, _basis, _first, _pulls, _weight_column, _weight_row,
     window, gram, basis, first, pulls, weight_column, weight_row, out, second, third, fourth,
 ):
     added, squares, trace = add_rim(
-        after, CORE + RIM, strip, root_column, ratio_column,
+        after, CORE + RIM, strip, ratio_column,
         window, gram, basis, first, pulls, weight_column, weight_row,
     )
     squares += sums[0:1, 0:1]
@@ -411,20 +408,20 @@
 
 def before_part(before, grown, sums, prepared):
     *grown, strip, sums = call(
-        before_kernel, "before_part", [vmem()] * 11,
+        before_kernel, "before_part", [vmem()] * 10,
         growing() + [shape(RIM, ROWS), shape(16, 128, dtype=F32)],
-        flops=2 * ROWS * RIM * (CORE + RIM), aliases={4 + k: k for k in range(7)},
-    )(before, sums, *prepared[:2], *grown)
+        flops=2 * ROWS * RIM * (CORE + RIM), aliases={3 + k: k for k in range(7)},
+    )(before, sums, prepared[1], *grown)
     return grown, strip, sums
 
 
 def analyse(after, grown, strip, state_mean, sums, prepared):
     chain = pltpu.VMEM((SPAN, CORE + 128), BF16)
     return call(
-        analyse_kernel, "analyse", [vmem()] * 13, growing() + [shape(ROWS, CORE)],
+        analyse_kernel, "analyse", [vmem()] * 12, growing() + [shape(ROWS, CORE)],
         scratch_shapes=[chain, chain, chain],
-        flops=8 * SPAN * SPAN * CORE, aliases={6 + k: k for k in range(7)},
-    )(after, strip, state_mean, sums, *prepared[:2], *grown)[-1]
+        flops=8 * SPAN * SPAN * CORE, aliases={5 + k: k for k in range(7)},
+    )(after, strip, state_mean, sums, prepared[1], *grown)[-1]
 
 
 def local(

time: 88.9 us -> 88.8 us (level)
  no operation moved by 1% of the time
where the time goes in v4:
time: 88.8 us; the launch traced here: 88.5 us
  blocking collectives  33.3 us (37%)
  starting transfers between devices  22.2 us (25%)
  waiting for transfers between devices  20.7 us (23%)
  Pallas kernels  11 us (12%)
  local copies, waits for them, and re-layouts  1.15 us (1%)
    all_to_all x1, blocking collectives, local(): lax.all_to_all(analysed, 'member', split_axis=0, concat_axis=0, tiled=True)  33.3 us
    all_to_all x1, waiting for transfers between devices, local(): lax.all_to_all(sent, 'member', split_axis=0, concat_axis=0, tiled=True)  17.9 us
    all_to_all x1, starting transfers between devices, local(): lax.all_to_all(sent, 'member', split_axis=0, concat_axis=0, tiled=True)  12.9 us
    ppermute x1, starting transfers between devices, local(): before = lax.ppermute(rightward, axes, up)  5.36 us
    pallas_call x1, Pallas kernels, analyse(): call(analyse_kernel, 'analyse', [vmem()] * 12, growing() + [shape(ROWS, C...  4.54 us
    ppermute x1, starting transfers between devices, local(): after = lax.ppermute(leftward, axes, down)  3.94 us
    ppermute x1, waiting for transfers between devices, local(): before = lax.ppermute(rightward, axes, up)  2.62 us
  transfers between devices with their start and end apart: 3, of which 3 were waited for; matrix products, arithmetic and copies ran while one was open for 0% of the time, Pallas kernels for 4%

profile of v4, /device:TPU:25, one launch (start us, length us, event | category | flops | bytes accessed | tf_op | source)
XLA Modules:
  0.0 88.5 jit_solution(7375659415589819941)
XLA Ops:
  0.0 0.0 copy-start
  0.0 1.1 %copy-done = bf16[32,30,384]{2,0,1:T(8,128)(2,1)S(1)} copy-done((bf16[32,30,384]{2,0,1:T(8,128)(2,1)S(1)}, bf16[32,30,384]{2,0,1:T(8,128)(2,1)}, u32[]{:S(2)}) %copy-start) | copy-done | bytes 737304
  1.1 0.0 copy-start.1
  1.1 0.0 copy-start.2
  1.1 0.0 copy-start.3
  1.1 0.0 copy-start.4
  1.1 0.0 copy-start.5
  1.1 0.0 copy-start.6
  1.1 0.0 copy-start.7
  1.2 1.3 %entry.1 = bf16[32,32,384]{2,1,0:T(8,128)(2,1)} custom-call(bf16[30,32,384]{2,1,0:T(8,128)(2,1)S(1)} %bitcast.7), custom_call_target="tpu_custom_call" | custom-call | flops 201326592 | bytes 1048576 | tf_op jit(solution)/shard_map/entry/pallas_call | solution.py:363
  2.5 12.9 %all-to-all-start = ((bf16[32,32,384]{2,1,0:T(8,128)(2,1)}), bf16[32,32,384]{2,1,0:T(8,128)(2,1)S(1)}, u32[]{:S(2)}, u32[]{:S(2)}) async-start(bf16[32,32,384]{2,1,0:T(8,128)(2,1)} %entry.1), calls=%async_computation | async-start | bytes 1572864 | tf_op jit(solution)/shard_map/all_to_all | solution.py:439
  15.4 0.0 copy-done.1
  15.4 0.0 copy-done.2
  15.4 0.0 copy-done.3
  15.4 0.0 copy-done.4
  15.4 0.0 copy-done.5
  15.4 0.0 copy-done.6
  15.4 0.0 copy-done.7
  15.5 1.3 %prepare.1 = (f32[768,128]{1,0:T(8,128)S(1)}, f32[768,128]{1,0:T(8,128)S(1)}, f32[8,768]{1,0:T(8,128)S(1)}, bf16[384,384]{1,0:T(8,128)(2,1)S(1)}) custom-call(s32[64]{0:T(128)S(1)} %copy-done.7, s32[32]{0:T(128)S(1)} %copy-done.5, s32[16]{0:T(128)S(1)} %copy-done.6, s32[32,640]{1,0:T(8,128)S(1)} %copy-done.1, f32[32,640]{1,0:T(8,128)S(1)} %copy-done.2, ...), custom_call_target="tpu_custom_call" | custom-call | flops 1966080 | bytes 1048576 | tf_op jit(solution)/shard_map/prepare/pallas_call | solution.py:377
  16.8 17.9 %all-to-all-done = bf16[32,32,384]{2,1,0:T(8,128)(2,1)S(1)} async-done(((bf16[32,32,384]{2,1,0:T(8,128)(2,1)}), bf16[32,32,384]{2,1,0:T(8,128)(2,1)S(1)}, u32[]{:S(2)}, u32[]{:S(2)}) %all-to-all-start) | async-done | bytes 786464 | tf_op jit(solution)/shard_map/all_to_all | solution.py:439
  34.6 0.6 extract.1
  35.2 5.4 %collective-permute-start.1 = (bf16[192,1024]{1,0:T(8,128)(2,1)S(1)}, bf16[192,1024]{1,0:T(8,128)(2,1)S(1)}, u32[]{:S(2)}, u32[]{:S(2)}) collective-permute-start(bf16[192,1024]{1,0:T(8,128)(2,1)S(1)} %get-tuple-element.32), channel_id=1, source_target_pairs={{0,128},{128,144},{144,272},{272,256},{256,368},{368,352},{352,224... | collective-permute-start | bytes 1179656 | tf_op jit(solution)/shard_map/ppermute | solution.py:449
  40.6 3.9 %collective-permute-start = (bf16[192,1024]{1,0:T(8,128)(2,1)S(1)}, bf16[192,1024]{1,0:T(8,128)(2,1)S(1)}, u32[]{:S(2)}, u32[]{:S(2)}) collective-permute-start(bf16[192,1024]{1,0:T(8,128)(2,1)S(1)} %get-tuple-element.31), channel_id=1, source_target_pairs={{128,0},{144,128},{272,144},{256,272},{368,256},{352,368},{224,352... | collective-permute-start | bytes 1179656 | tf_op jit(solution)/shard_map/ppermute | solution.py:450
  44.6 1.2 %own_part.1 = (bf16[1024,768]{1,0:T(8,128)(2,1)S(1)}, bf16[768,768]{1,0:T(8,128)(2,1)S(1)}, f32[768,384]{1,0:T(8,128)S(1)}, bf16[768,512]{1,0:T(8,128)(2,1)S(1)}...) custom-call(bf16[1024,384]{1,0:T(8,128)(2,1)S(1)} %bitcast.5, ...), custom_call_target="tpu_custom_call" | custom-call | flops 301989888 | bytes 1048576 | tf_op jit(solution)/shard_map/own_part/pallas_call | solution.py:401
  45.8 2.6 %collective-permute-done.1.before = bf16[192,1024]{1,0:T(8,128)(2,1)S(1)} collective-permute-done((bf16[192,1024]{1,0:T(8,128)(2,1)S(1)}, bf16[192,1024]{1,0:T(8,128)(2,1)S(1)}, u32[]{:S(2)}, u32[]{:S(2)}) %collective-permute-start.1) | collective-permute-done | bytes 393248 | tf_op jit(solution)/shard_map/ppermute | solution.py:449
  48.4 0.8 before_part.1
  49.2 0.2 collective-permute-done.after
  49.4 4.5 %analyse.1 = (bf16[1024,768]{1,0:T(8,128)(2,1)S(1)}, bf16[768,768]{1,0:T(8,128)(2,1)S(1)}, f32[768,384]{1,0:T(8,128)S(1)}, bf16[768,512]{1,0:T(8,128)(2,1)S(1)},...) custom-call(bf16[192,1024]{1,0:T(8,128)(2,1)S(1)} %collective-permut, ...), custom_call_target="tpu_custom_call", output_to_operand_aliasing={{0}: (5, {}), {1}: (6, {}), {2}: (7, {}), {3}: (8, {}), {4}... | custom-call | flops 1811939328 | bytes 1048576 | tf_op jit(solution)/shard_map/analyse/pallas_call | solution.py:420
  54.0 33.3 %all_to_all.10.analysed = bf16[32,32,384]{2,1,0:T(8,128)(2,1)S(1)} all-to-all(bf16[32,32,384]{2,1,0:T(8,128)(2,1)S(1)} %bitcast.6), channel_id=1, replica_groups=mesh['member'=32,'patch'=16] {'member'}, dimensions={0} | all-to-all | bytes 1572864 | tf_op jit(solution)/shard_map/all_to_all | solution.py:455
  87.3 1.2 %exit.1 = bf16[30,32,384]{2,1,0:T(8,128)(2,1)} custom-call(bf16[32,32,384]{2,1,0:T(8,128)(2,1)S(1)} %all_to_all.10.analysed), custom_call_target="tpu_custom_call" | custom-call | flops 201326592 | bytes 1048576 | tf_op jit(solution)/shard_map/exit/pallas_call | solution.py:369
Async XLA Ops:
  0.0 1.1 %copy-start = (bf16[32,30,384]{2,0,1:T(8,128)(2,1)S(1)}, bf16[32,30,384]{2,0,1:T(8,128)(2,1)}, u32[]{:S(2)}) copy-start(bf16[32,30,384]{2,0,1:T(8,128)(2,1)} %param.8) | copy-start | bytes 2211844
  1.1 14.3 %copy-start.1 = (s32[32,640]{1,0:T(8,128)S(1)}, s32[32,640]{1,0:T(8,128)}, u32[]{:S(2)}) copy-start(s32[32,640]{1,0:T(8,128)} %location.1) | copy-start | bytes 245764
  1.1 14.3 %copy-start.2 = (f32[32,640]{1,0:T(8,128)S(1)}, f32[32,640]{1,0:T(8,128)}, u32[]{:S(2)}) copy-start(f32[32,640]{1,0:T(8,128)} %datum.1) | copy-start | bytes 245764
  1.1 14.3 %copy-start.3 = (f32[32,640]{1,0:T(8,128)S(1)}, f32[32,640]{1,0:T(8,128)}, u32[]{:S(2)}) copy-start(f32[32,640]{1,0:T(8,128)} %error_spread.1) | copy-start | bytes 245764
  1.1 14.3 %copy-start.4 = (s32[32,640]{1,0:T(8,128)S(1)}, s32[32,640]{1,0:T(8,128)}, u32[]{:S(2)}) copy-start(s32[32,640]{1,0:T(8,128)} %band.1) | copy-start | bytes 245764
  1.1 14.3 %copy-start.5 = (s32[32]{0:T(128)S(1)}, s32[32]{0:T(128)}, u32[]{:S(2)}) copy-start(s32[32]{0:T(128)} %tally.1) | copy-start | bytes 388
  1.1 14.3 %copy-start.6 = (s32[16]{0:T(128)S(1)}, s32[16]{0:T(128)}, u32[]{:S(2)}) copy-start(s32[16]{0:T(128)} %taper.1) | copy-start | bytes 196
  1.1 14.3 %copy-start.7 = (s32[64]{0:T(128)S(1)}, s32[64]{0:T(128)}, u32[]{:S(2)}) copy-start(s32[64]{0:T(128)} %constant.2.clone.hosted) | copy-start | bytes 772
  2.5 32.1 %all-to-all-start = ((bf16[32,32,384]{2,1,0:T(8,128)(2,1)}), bf16[32,32,384]{2,1,0:T(8,128)(2,1)S(1)}, u32[]{:S(2)}, u32[]{:S(2)}) async-start(bf16[32,32,384]{2,1,0:T(8,128)(2,1)} %entry.1), calls=%async_computation | async-start | bytes 1572864 | tf_op jit(solution)/shard_map/all_to_all | solution.py:439
  35.2 13.1 %collective-permute-start.1 = (bf16[192,1024]{1,0:T(8,128)(2,1)S(1)}, bf16[192,1024]{1,0:T(8,128)(2,1)S(1)}, u32[]{:S(2)}, u32[]{:S(2)}) collective-permute-start(bf16[192,1024]{1,0:T(8,128)(2,1)S(1)} %get-tuple-element.32), channel_id=1, source_target_pairs={{0,128},{128,144},{144,272},{272,256},{256,368},{368,352},{352,224... | collective-permute-start | bytes 1179656 | tf_op jit(solution)/shard_map/ppermute | solution.py:449
  40.6 8.8 %collective-permute-start = (bf16[192,1024]{1,0:T(8,128)(2,1)S(1)}, bf16[192,1024]{1,0:T(8,128)(2,1)S(1)}, u32[]{:S(2)}, u32[]{:S(2)}) collective-permute-start(bf16[192,1024]{1,0:T(8,128)(2,1)S(1)} %get-tuple-element.31), channel_id=1, source_target_pairs={{128,0},{144,128},{272,144},{256,272},{368,256},{352,368},{224,352... | collective-permute-start | bytes 1179656 | tf_op jit(solution)/shard_map/ppermute | solution.py:450

commit v5 on v4

--- a/solution.py
+++ b/solution.py
@@ -108,12 +108,12 @@
             count = min(EIGHT, HELD - first)
             block = jnp.concatenate([tile[k * EIGHT : (k + 1) * EIGHT, :] for tile in tiles], axis=0)
             moved = mm(swap[: count * GROUP, :], block.astype(BF16)).astype(BF16)
-            buffer[first : first + count] = moved.reshape(count, GROUP, CORE)
-        rows = slice(start, min(start + 2 * EIGHT, HELD))
-        copies.append(
-            pltpu.make_async_copy(buffer.at[rows], out.at[rows], sent.at[start // (2 * EIGHT)])
-        )
-        copies[-1].start()
+            rows = slice(first, first + count)
+            buffer[rows] = moved.reshape(count, GROUP, CORE)
+            copies.append(
+                pltpu.make_async_copy(buffer.at[rows], out.at[rows], sent.at[first // EIGHT])
+            )
+            copies[-1].start()
     for copy in copies:
         copy.wait()
 
@@ -368,7 +368,7 @@
 def leave(analysed):
     return call(
         exit_kernel, "exit", [vmem()], shape(HELD, GROUP, CORE), hbm(),
-        [pltpu.VMEM((HELD, GROUP, CORE), BF16), pltpu.SemaphoreType.DMA((2,))],
+        [pltpu.VMEM((HELD, GROUP, CORE), BF16), pltpu.SemaphoreType.DMA((4,))],
         8 * 256 * 256 * CORE,
     )(analysed)
 

time: 88.8 us -> 88.7 us (level)
  no operation moved by 1% of the time
where the time goes in v5:
time: 88.7 us; the launch traced here: 88.4 us
  blocking collectives  33.3 us (38%)
  starting transfers between devices  22.2 us (25%)
  waiting for transfers between devices  20.7 us (23%)
  Pallas kernels  11 us (12%)
  local copies, waits for them, and re-layouts  1.15 us (1%)
    all_to_all x1, blocking collectives, local(): lax.all_to_all(analysed, 'member', split_axis=0, concat_axis=0, tiled=True)  33.3 us
    all_to_all x1, waiting for transfers between devices, local(): lax.all_to_all(sent, 'member', split_axis=0, concat_axis=0, tiled=True)  17.9 us
    all_to_all x1, starting transfers between devices, local(): lax.all_to_all(sent, 'member', split_axis=0, concat_axis=0, tiled=True)  12.9 us
    ppermute x1, starting transfers between devices, local(): before = lax.ppermute(rightward, axes, up)  5.36 us
    pallas_call x1, Pallas kernels, analyse(): call(analyse_kernel, 'analyse', [vmem()] * 12, growing() + [shape(ROWS, C...  4.54 us
    ppermute x1, starting transfers between devices, local(): after = lax.ppermute(leftward, axes, down)  3.94 us
    ppermute x1, waiting for transfers between devices, local(): before = lax.ppermute(rightward, axes, up)  2.62 us
  transfers between devices with their start and end apart: 3, of which 3 were waited for; matrix products, arithmetic and copies ran while one was open for 0% of the time, Pallas kernels for 4%

profile of v5, /device:TPU:25, one launch (start us, length us, event | category | flops | bytes accessed | tf_op | source)
XLA Modules:
  0.0 88.4 jit_solution(6158721060074150529)
XLA Ops:
  0.0 0.0 copy-start
  0.0 1.1 %copy-done = bf16[32,30,384]{2,0,1:T(8,128)(2,1)S(1)} copy-done((bf16[32,30,384]{2,0,1:T(8,128)(2,1)S(1)}, bf16[32,30,384]{2,0,1:T(8,128)(2,1)}, u32[]{:S(2)}) %copy-start) | copy-done | bytes 737304
  1.1 0.0 copy-start.1
  1.1 0.0 copy-start.2
  1.1 0.0 copy-start.3
  1.1 0.0 copy-start.4
  1.1 0.0 copy-start.5
  1.1 0.0 copy-start.6
  1.1 0.0 copy-start.7
  1.2 1.3 %entry.1 = bf16[32,32,384]{2,1,0:T(8,128)(2,1)} custom-call(bf16[30,32,384]{2,1,0:T(8,128)(2,1)S(1)} %bitcast.7), custom_call_target="tpu_custom_call" | custom-call | flops 201326592 | bytes 1048576 | tf_op jit(solution)/shard_map/entry/pallas_call | solution.py:363
  2.5 12.9 %all-to-all-start = ((bf16[32,32,384]{2,1,0:T(8,128)(2,1)}), bf16[32,32,384]{2,1,0:T(8,128)(2,1)S(1)}, u32[]{:S(2)}, u32[]{:S(2)}) async-start(bf16[32,32,384]{2,1,0:T(8,128)(2,1)} %entry.1), calls=%async_computation | async-start | bytes 1572864 | tf_op jit(solution)/shard_map/all_to_all | solution.py:439
  15.4 0.0 copy-done.1
  15.4 0.0 copy-done.2
  15.4 0.0 copy-done.3
  15.4 0.0 copy-done.4
  15.4 0.0 copy-done.5
  15.4 0.0 copy-done.6
  15.4 0.0 copy-done.7
  15.5 1.3 %prepare.1 = (f32[768,128]{1,0:T(8,128)S(1)}, f32[768,128]{1,0:T(8,128)S(1)}, f32[8,768]{1,0:T(8,128)S(1)}, bf16[384,384]{1,0:T(8,128)(2,1)S(1)}) custom-call(s32[64]{0:T(128)S(1)} %copy-done.7, s32[32]{0:T(128)S(1)} %copy-done.5, s32[16]{0:T(128)S(1)} %copy-done.6, s32[32,640]{1,0:T(8,128)S(1)} %copy-done.1, f32[32,640]{1,0:T(8,128)S(1)} %copy-done.2, ...), custom_call_target="tpu_custom_call" | custom-call | flops 1966080 | bytes 1048576 | tf_op jit(solution)/shard_map/prepare/pallas_call | solution.py:377
  16.8 17.9 %all-to-all-done = bf16[32,32,384]{2,1,0:T(8,128)(2,1)S(1)} async-done(((bf16[32,32,384]{2,1,0:T(8,128)(2,1)}), bf16[32,32,384]{2,1,0:T(8,128)(2,1)S(1)}, u32[]{:S(2)}, u32[]{:S(2)}) %all-to-all-start) | async-done | bytes 786464 | tf_op jit(solution)/shard_map/all_to_all | solution.py:439
  34.6 0.6 extract.1
  35.2 5.4 %collective-permute-start.1 = (bf16[192,1024]{1,0:T(8,128)(2,1)S(1)}, bf16[192,1024]{1,0:T(8,128)(2,1)S(1)}, u32[]{:S(2)}, u32[]{:S(2)}) collective-permute-start(bf16[192,1024]{1,0:T(8,128)(2,1)S(1)} %get-tuple-element.32), channel_id=1, source_target_pairs={{0,128},{128,144},{144,272},{272,256},{256,368},{368,352},{352,224... | collective-permute-start | bytes 1179656 | tf_op jit(solution)/shard_map/ppermute | solution.py:449
  40.6 3.9 %collective-permute-start = (bf16[192,1024]{1,0:T(8,128)(2,1)S(1)}, bf16[192,1024]{1,0:T(8,128)(2,1)S(1)}, u32[]{:S(2)}, u32[]{:S(2)}) collective-permute-start(bf16[192,1024]{1,0:T(8,128)(2,1)S(1)} %get-tuple-element.31), channel_id=1, source_target_pairs={{128,0},{144,128},{272,144},{256,272},{368,256},{352,368},{224,352... | collective-permute-start | bytes 1179656 | tf_op jit(solution)/shard_map/ppermute | solution.py:450
  44.6 1.2 %own_part.1 = (bf16[1024,768]{1,0:T(8,128)(2,1)S(1)}, bf16[768,768]{1,0:T(8,128)(2,1)S(1)}, f32[768,384]{1,0:T(8,128)S(1)}, bf16[768,512]{1,0:T(8,128)(2,1)S(1)}...) custom-call(bf16[1024,384]{1,0:T(8,128)(2,1)S(1)} %bitcast.5, ...), custom_call_target="tpu_custom_call" | custom-call | flops 301989888 | bytes 1048576 | tf_op jit(solution)/shard_map/own_part/pallas_call | solution.py:401
  45.8 2.6 %collective-permute-done.1.before = bf16[192,1024]{1,0:T(8,128)(2,1)S(1)} collective-permute-done((bf16[192,1024]{1,0:T(8,128)(2,1)S(1)}, bf16[192,1024]{1,0:T(8,128)(2,1)S(1)}, u32[]{:S(2)}, u32[]{:S(2)}) %collective-permute-start.1) | collective-permute-done | bytes 393248 | tf_op jit(solution)/shard_map/ppermute | solution.py:449
  48.4 0.8 before_part.1
  49.2 0.2 collective-permute-done.after
  49.4 4.5 %analyse.1 = (bf16[1024,768]{1,0:T(8,128)(2,1)S(1)}, bf16[768,768]{1,0:T(8,128)(2,1)S(1)}, f32[768,384]{1,0:T(8,128)S(1)}, bf16[768,512]{1,0:T(8,128)(2,1)S(1)},...) custom-call(bf16[192,1024]{1,0:T(8,128)(2,1)S(1)} %collective-permut, ...), custom_call_target="tpu_custom_call", output_to_operand_aliasing={{0}: (5, {}), {1}: (6, {}), {2}: (7, {}), {3}: (8, {}), {4}... | custom-call | flops 1811939328 | bytes 1048576 | tf_op jit(solution)/shard_map/analyse/pallas_call | solution.py:420
  54.0 33.3 %all_to_all.10.analysed = bf16[32,32,384]{2,1,0:T(8,128)(2,1)S(1)} all-to-all(bf16[32,32,384]{2,1,0:T(8,128)(2,1)S(1)} %bitcast.6), channel_id=1, replica_groups=mesh['member'=32,'patch'=16] {'member'}, dimensions={0} | all-to-all | bytes 1572864 | tf_op jit(solution)/shard_map/all_to_all | solution.py:455
  87.3 1.2 %exit.1 = bf16[30,32,384]{2,1,0:T(8,128)(2,1)} custom-call(bf16[32,32,384]{2,1,0:T(8,128)(2,1)S(1)} %all_to_all.10.analysed), custom_call_target="tpu_custom_call" | custom-call | flops 201326592 | bytes 1048576 | tf_op jit(solution)/shard_map/exit/pallas_call | solution.py:369
Async XLA Ops:
  0.0 1.1 %copy-start = (bf16[32,30,384]{2,0,1:T(8,128)(2,1)S(1)}, bf16[32,30,384]{2,0,1:T(8,128)(2,1)}, u32[]{:S(2)}) copy-start(bf16[32,30,384]{2,0,1:T(8,128)(2,1)} %param.8) | copy-start | bytes 2211844
  1.1 14.3 %copy-start.1 = (s32[32,640]{1,0:T(8,128)S(1)}, s32[32,640]{1,0:T(8,128)}, u32[]{:S(2)}) copy-start(s32[32,640]{1,0:T(8,128)} %location.1) | copy-start | bytes 245764
  1.1 14.3 %copy-start.2 = (f32[32,640]{1,0:T(8,128)S(1)}, f32[32,640]{1,0:T(8,128)}, u32[]{:S(2)}) copy-start(f32[32,640]{1,0:T(8,128)} %datum.1) | copy-start | bytes 245764
  1.1 14.3 %copy-start.3 = (f32[32,640]{1,0:T(8,128)S(1)}, f32[32,640]{1,0:T(8,128)}, u32[]{:S(2)}) copy-start(f32[32,640]{1,0:T(8,128)} %error_spread.1) | copy-start | bytes 245764
  1.1 14.3 %copy-start.4 = (s32[32,640]{1,0:T(8,128)S(1)}, s32[32,640]{1,0:T(8,128)}, u32[]{:S(2)}) copy-start(s32[32,640]{1,0:T(8,128)} %band.1) | copy-start | bytes 245764
  1.1 14.3 %copy-start.5 = (s32[32]{0:T(128)S(1)}, s32[32]{0:T(128)}, u32[]{:S(2)}) copy-start(s32[32]{0:T(128)} %tally.1) | copy-start | bytes 388
  1.1 14.3 %copy-start.6 = (s32[16]{0:T(128)S(1)}, s32[16]{0:T(128)}, u32[]{:S(2)}) copy-start(s32[16]{0:T(128)} %taper.1) | copy-start | bytes 196
  1.1 14.3 %copy-start.7 = (s32[64]{0:T(128)S(1)}, s32[64]{0:T(128)}, u32[]{:S(2)}) copy-start(s32[64]{0:T(128)} %constant.2.clone.hosted) | copy-start | bytes 772
  2.5 32.1 %all-to-all-start = ((bf16[32,32,384]{2,1,0:T(8,128)(2,1)}), bf16[32,32,384]{2,1,0:T(8,128)(2,1)S(1)}, u32[]{:S(2)}, u32[]{:S(2)}) async-start(bf16[32,32,384]{2,1,0:T(8,128)(2,1)} %entry.1), calls=%async_computation | async-start | bytes 1572864 | tf_op jit(solution)/shard_map/all_to_all | solution.py:439
  35.2 13.1 %collective-permute-start.1 = (bf16[192,1024]{1,0:T(8,128)(2,1)S(1)}, bf16[192,1024]{1,0:T(8,128)(2,1)S(1)}, u32[]{:S(2)}, u32[]{:S(2)}) collective-permute-start(bf16[192,1024]{1,0:T(8,128)(2,1)S(1)} %get-tuple-element.32), channel_id=1, source_target_pairs={{0,128},{128,144},{144,272},{272,256},{256,368},{368,352},{352,224... | collective-permute-start | bytes 1179656 | tf_op jit(solution)/shard_map/ppermute | solution.py:449
  40.6 8.8 %collective-permute-start = (bf16[192,1024]{1,0:T(8,128)(2,1)S(1)}, bf16[192,1024]{1,0:T(8,128)(2,1)S(1)}, u32[]{:S(2)}, u32[]{:S(2)}) collective-permute-start(bf16[192,1024]{1,0:T(8,128)(2,1)S(1)} %get-tuple-element.31), channel_id=1, source_target_pairs={{128,0},{144,128},{272,144},{256,272},{368,256},{352,368},{224,352... | collective-permute-start | bytes 1179656 | tf_op jit(solution)/shard_map/ppermute | solution.py:450

commit v6 on v5

--- a/solution.py
+++ b/solution.py
@@ -320,10 +320,11 @@
             fourth[:, last] = (1.5 * pulls[...] + x).astype(BF16)
 
     chain = (first, second, third, fourth)
-    waiting = [product(first, 0), product(first, 1)]
+    late = product(first, 1)
+    waiting = [product(first, 0), late]
     window[:, CORE + RIM :] = added.T
     for k, finish in enumerate((one, two, three)):
-        for h in range(2):
+        for h in (1, 0):
             finish(h, waiting[h])
             waiting[h] = product(chain[k + 1], h)
     x = r * fourth[:, last].astype(F32) - (0.5 * inverse) * waiting[1][:, 128:]

time: 88.7 us -> 88.7 us (level)
  no operation moved by 1% of the time
where the time goes in v6:
time: 88.7 us; the launch traced here: 88.4 us
  blocking collectives  33.3 us (38%)
  starting transfers between devices  22.2 us (25%)
  waiting for transfers between devices  20.7 us (23%)
  Pallas kernels  11 us (12%)
  local copies, waits for them, and re-layouts  1.15 us (1%)
    all_to_all x1, blocking collectives, local(): lax.all_to_all(analysed, 'member', split_axis=0, concat_axis=0, tiled=True)  33.3 us
    all_to_all x1, waiting for transfers between devices, local(): lax.all_to_all(sent, 'member', split_axis=0, concat_axis=0, tiled=True)  17.9 us
    all_to_all x1, starting transfers between devices, local(): lax.all_to_all(sent, 'member', split_axis=0, concat_axis=0, tiled=True)  12.9 us
    ppermute x1, starting transfers between devices, local(): before = lax.ppermute(rightward, axes, up)  5.36 us
    pallas_call x1, Pallas kernels, analyse(): call(analyse_kernel, 'analyse', [vmem()] * 12, growing() + [shape(ROWS, C...  4.54 us
    ppermute x1, starting transfers between devices, local(): after = lax.ppermute(leftward, axes, down)  3.94 us
    ppermute x1, waiting for transfers between devices, local(): before = lax.ppermute(rightward, axes, up)  2.62 us
  transfers between devices with their start and end apart: 3, of which 3 were waited for; matrix products, arithmetic and copies ran while one was open for 0% of the time, Pallas kernels for 4%

profile of v6, /device:TPU:25, one launch (start us, length us, event | category | flops | bytes accessed | tf_op | source)
XLA Modules:
  0.0 88.4 jit_solution(15062705082748970601)
XLA Ops:
  0.0 0.0 copy-start
  0.0 1.1 %copy-done = bf16[32,30,384]{2,0,1:T(8,128)(2,1)S(1)} copy-done((bf16[32,30,384]{2,0,1:T(8,128)(2,1)S(1)}, bf16[32,30,384]{2,0,1:T(8,128)(2,1)}, u32[]{:S(2)}) %copy-start) | copy-done | bytes 737304
  1.1 0.0 copy-start.1
  1.1 0.0 copy-start.2
  1.1 0.0 copy-start.3
  1.1 0.0 copy-start.4
  1.1 0.0 copy-start.5
  1.1 0.0 copy-start.6
  1.1 0.0 copy-start.7
  1.2 1.3 %entry.1 = bf16[32,32,384]{2,1,0:T(8,128)(2,1)} custom-call(bf16[30,32,384]{2,1,0:T(8,128)(2,1)S(1)} %bitcast.7), custom_call_target="tpu_custom_call" | custom-call | flops 201326592 | bytes 1048576 | tf_op jit(solution)/shard_map/entry/pallas_call | solution.py:364
  2.5 12.9 %all-to-all-start = ((bf16[32,32,384]{2,1,0:T(8,128)(2,1)}), bf16[32,32,384]{2,1,0:T(8,128)(2,1)S(1)}, u32[]{:S(2)}, u32[]{:S(2)}) async-start(bf16[32,32,384]{2,1,0:T(8,128)(2,1)} %entry.1), calls=%async_computation | async-start | bytes 1572864 | tf_op jit(solution)/shard_map/all_to_all | solution.py:440
  15.4 0.0 copy-done.1
  15.4 0.0 copy-done.2
  15.4 0.0 copy-done.3
  15.4 0.0 copy-done.4
  15.4 0.0 copy-done.5
  15.4 0.0 copy-done.6
  15.4 0.0 copy-done.7
  15.5 1.3 %prepare.1 = (f32[768,128]{1,0:T(8,128)S(1)}, f32[768,128]{1,0:T(8,128)S(1)}, f32[8,768]{1,0:T(8,128)S(1)}, bf16[384,384]{1,0:T(8,128)(2,1)S(1)}) custom-call(s32[64]{0:T(128)S(1)} %copy-done.7, s32[32]{0:T(128)S(1)} %copy-done.5, s32[16]{0:T(128)S(1)} %copy-done.6, s32[32,640]{1,0:T(8,128)S(1)} %copy-done.1, f32[32,640]{1,0:T(8,128)S(1)} %copy-done.2, ...), custom_call_target="tpu_custom_call" | custom-call | flops 1966080 | bytes 1048576 | tf_op jit(solution)/shard_map/prepare/pallas_call | solution.py:378
  16.8 17.9 %all-to-all-done = bf16[32,32,384]{2,1,0:T(8,128)(2,1)S(1)} async-done(((bf16[32,32,384]{2,1,0:T(8,128)(2,1)}), bf16[32,32,384]{2,1,0:T(8,128)(2,1)S(1)}, u32[]{:S(2)}, u32[]{:S(2)}) %all-to-all-start) | async-done | bytes 786464 | tf_op jit(solution)/shard_map/all_to_all | solution.py:440
  34.6 0.6 extract.1
  35.2 5.4 %collective-permute-start.1 = (bf16[192,1024]{1,0:T(8,128)(2,1)S(1)}, bf16[192,1024]{1,0:T(8,128)(2,1)S(1)}, u32[]{:S(2)}, u32[]{:S(2)}) collective-permute-start(bf16[192,1024]{1,0:T(8,128)(2,1)S(1)} %get-tuple-element.32), channel_id=1, source_target_pairs={{0,128},{128,144},{144,272},{272,256},{256,368},{368,352},{352,224... | collective-permute-start | bytes 1179656 | tf_op jit(solution)/shard_map/ppermute | solution.py:450
  40.6 3.9 %collective-permute-start = (bf16[192,1024]{1,0:T(8,128)(2,1)S(1)}, bf16[192,1024]{1,0:T(8,128)(2,1)S(1)}, u32[]{:S(2)}, u32[]{:S(2)}) collective-permute-start(bf16[192,1024]{1,0:T(8,128)(2,1)S(1)} %get-tuple-element.31), channel_id=1, source_target_pairs={{128,0},{144,128},{272,144},{256,272},{368,256},{352,368},{224,352... | collective-permute-start | bytes 1179656 | tf_op jit(solution)/shard_map/ppermute | solution.py:451
  44.6 1.2 %own_part.1 = (bf16[1024,768]{1,0:T(8,128)(2,1)S(1)}, bf16[768,768]{1,0:T(8,128)(2,1)S(1)}, f32[768,384]{1,0:T(8,128)S(1)}, bf16[768,512]{1,0:T(8,128)(2,1)S(1)}...) custom-call(bf16[1024,384]{1,0:T(8,128)(2,1)S(1)} %bitcast.5, ...), custom_call_target="tpu_custom_call" | custom-call | flops 301989888 | bytes 1048576 | tf_op jit(solution)/shard_map/own_part/pallas_call | solution.py:402
  45.8 2.6 %collective-permute-done.1.before = bf16[192,1024]{1,0:T(8,128)(2,1)S(1)} collective-permute-done((bf16[192,1024]{1,0:T(8,128)(2,1)S(1)}, bf16[192,1024]{1,0:T(8,128)(2,1)S(1)}, u32[]{:S(2)}, u32[]{:S(2)}) %collective-permute-start.1) | collective-permute-done | bytes 393248 | tf_op jit(solution)/shard_map/ppermute | solution.py:450
  48.4 0.8 before_part.1
  49.2 0.2 collective-permute-done.after
  49.4 4.5 %analyse.1 = (bf16[1024,768]{1,0:T(8,128)(2,1)S(1)}, bf16[768,768]{1,0:T(8,128)(2,1)S(1)}, f32[768,384]{1,0:T(8,128)S(1)}, bf16[768,512]{1,0:T(8,128)(2,1)S(1)},...) custom-call(bf16[192,1024]{1,0:T(8,128)(2,1)S(1)} %collective-permut, ...), custom_call_target="tpu_custom_call", output_to_operand_aliasing={{0}: (5, {}), {1}: (6, {}), {2}: (7, {}), {3}: (8, {}), {4}... | custom-call | flops 1811939328 | bytes 1048576 | tf_op jit(solution)/shard_map/analyse/pallas_call | solution.py:421
  54.0 33.3 %all_to_all.10.analysed = bf16[32,32,384]{2,1,0:T(8,128)(2,1)S(1)} all-to-all(bf16[32,32,384]{2,1,0:T(8,128)(2,1)S(1)} %bitcast.6), channel_id=1, replica_groups=mesh['member'=32,'patch'=16] {'member'}, dimensions={0} | all-to-all | bytes 1572864 | tf_op jit(solution)/shard_map/all_to_all | solution.py:456
  87.2 1.2 %exit.1 = bf16[30,32,384]{2,1,0:T(8,128)(2,1)} custom-call(bf16[32,32,384]{2,1,0:T(8,128)(2,1)S(1)} %all_to_all.10.analysed), custom_call_target="tpu_custom_call" | custom-call | flops 201326592 | bytes 1048576 | tf_op jit(solution)/shard_map/exit/pallas_call | solution.py:370
Async XLA Ops:
  0.0 1.1 %copy-start = (bf16[32,30,384]{2,0,1:T(8,128)(2,1)S(1)}, bf16[32,30,384]{2,0,1:T(8,128)(2,1)}, u32[]{:S(2)}) copy-start(bf16[32,30,384]{2,0,1:T(8,128)(2,1)} %param.8) | copy-start | bytes 2211844
  1.1 14.3 %copy-start.1 = (s32[32,640]{1,0:T(8,128)S(1)}, s32[32,640]{1,0:T(8,128)}, u32[]{:S(2)}) copy-start(s32[32,640]{1,0:T(8,128)} %location.1) | copy-start | bytes 245764
  1.1 14.3 %copy-start.2 = (f32[32,640]{1,0:T(8,128)S(1)}, f32[32,640]{1,0:T(8,128)}, u32[]{:S(2)}) copy-start(f32[32,640]{1,0:T(8,128)} %datum.1) | copy-start | bytes 245764
  1.1 14.3 %copy-start.3 = (f32[32,640]{1,0:T(8,128)S(1)}, f32[32,640]{1,0:T(8,128)}, u32[]{:S(2)}) copy-start(f32[32,640]{1,0:T(8,128)} %error_spread.1) | copy-start | bytes 245764
  1.1 14.3 %copy-start.4 = (s32[32,640]{1,0:T(8,128)S(1)}, s32[32,640]{1,0:T(8,128)}, u32[]{:S(2)}) copy-start(s32[32,640]{1,0:T(8,128)} %band.1) | copy-start | bytes 245764
  1.1 14.3 %copy-start.5 = (s32[32]{0:T(128)S(1)}, s32[32]{0:T(128)}, u32[]{:S(2)}) copy-start(s32[32]{0:T(128)} %tally.1) | copy-start | bytes 388
  1.1 14.3 %copy-start.6 = (s32[16]{0:T(128)S(1)}, s32[16]{0:T(128)}, u32[]{:S(2)}) copy-start(s32[16]{0:T(128)} %taper.1) | copy-start | bytes 196
  1.1 14.3 %copy-start.7 = (s32[64]{0:T(128)S(1)}, s32[64]{0:T(128)}, u32[]{:S(2)}) copy-start(s32[64]{0:T(128)} %constant.2.clone.hosted) | copy-start | bytes 772
  2.5 32.1 %all-to-all-start = ((bf16[32,32,384]{2,1,0:T(8,128)(2,1)}), bf16[32,32,384]{2,1,0:T(8,128)(2,1)S(1)}, u32[]{:S(2)}, u32[]{:S(2)}) async-start(bf16[32,32,384]{2,1,0:T(8,128)(2,1)} %entry.1), calls=%async_computation | async-start | bytes 1572864 | tf_op jit(solution)/shard_map/all_to_all | solution.py:440
  35.2 13.1 %collective-permute-start.1 = (bf16[192,1024]{1,0:T(8,128)(2,1)S(1)}, bf16[192,1024]{1,0:T(8,128)(2,1)S(1)}, u32[]{:S(2)}, u32[]{:S(2)}) collective-permute-start(bf16[192,1024]{1,0:T(8,128)(2,1)S(1)} %get-tuple-element.32), channel_id=1, source_target_pairs={{0,128},{128,144},{144,272},{272,256},{256,368},{368,352},{352,224... | collective-permute-start | bytes 1179656 | tf_op jit(solution)/shard_map/ppermute | solution.py:450
  40.6 8.8 %collective-permute-start = (bf16[192,1024]{1,0:T(8,128)(2,1)S(1)}, bf16[192,1024]{1,0:T(8,128)(2,1)S(1)}, u32[]{:S(2)}, u32[]{:S(2)}) collective-permute-start(bf16[192,1024]{1,0:T(8,128)(2,1)S(1)} %get-tuple-element.31), channel_id=1, source_target_pairs={{128,0},{144,128},{272,144},{256,272},{368,256},{352,368},{224,352... | collective-permute-start | bytes 1179656 | tf_op jit(solution)/shard_map/ppermute | solution.py:451
